TPU v7x, 256 devices: a whole 4x4x8 slice. The times are simulated.
256 devices in a mesh: dp: 16 (over y_lo, x, core), feat: 16 (over z, y_hi).
Axes of the slice: x: 4, y: 4 (y_hi: 2, y_lo: 2; y = y_hi * 2 + y_lo), z: 8, core: 2. Of those that a mesh axis runs over, the one named last changes fastest.
Arguments:
- view_one: bfloat16 [3840, 8192], P('dp', 'feat'), may hold values from -25 to 25
- view_two: bfloat16 [3840, 8192], P('feat', 'dp'), may hold values from -25 to 25
- inputs_one: bfloat16 [3840, 8192], P(None, 'dp'), may hold values from -6 to 6
- inputs_two: bfloat16 [3840, 8192], P(None, 'feat'), may hold values from -6 to 6
- loss_scale: float32 [1], replicated, may hold values from 32 to 128
Outputs:
- loss_value: float32 [1], replicated
- weight_grad_one: float32 [8192, 8192], P('dp', 'feat')
- weight_grad_two: float32 [8192, 8192], P('feat', 'dp')
All inputs are finite; a program needn't handle non-finite values.
Results may differ from a plain program's by a relative error of at most 0.0075.
Values may be sent and summed in bfloat16 or wider, within the bound.
A program may use at most 128 MiB of HBM per device.

v0:
```python
import jax
import jax.numpy as jnp
from jax import lax
from jax.sharding import PartitionSpec as P

F = 8192


off_weight = 0.0051
epsilon = 1e-05


def column_moments(block):
    values = block.astype(jnp.float32)
    return (jnp.sum(values, axis=0), jnp.sum(values * values, axis=0))


def finish(sums, squares, batch_rows):
    average = sums / batch_rows
    spread = squares / batch_rows - average * average
    return (average, lax.rsqrt(spread + epsilon))


def standardize(block, average, inv_std):
    return ((block.astype(jnp.float32) - average) * inv_std).astype(jnp.bfloat16)


def apply_delta(upstream, normed, inv_std, first, second, batch_rows):
    own = normed.astype(jnp.float32)
    return (inv_std * (upstream - first / batch_rows - own * second / batch_rows)).astype(
        jnp.bfloat16
    )


def contract_rows(left, right):
    return lax.dot_general(
        left, right, (((0,), (0,)), ((), ())), preferred_element_type=jnp.float32
    )


def per_device(view_one, view_two, inputs_one, inputs_two, loss_scale):
    rows_one = view_one.shape[0]
    batch_rows = rows_one * lax.axis_size("dp")
    sums_one, squares_one = column_moments(view_one)
    sums_one, squares_one = lax.psum((sums_one, squares_one), "dp")
    average_one, inv_one = finish(sums_one, squares_one, batch_rows)
    sums_two, squares_two = column_moments(view_two)
    sums_two, squares_two = lax.psum((sums_two, squares_two), "feat")
    average_two, inv_two = finish(sums_two, squares_two, batch_rows)
    sent_one = standardize(view_one, average_one, inv_one)
    sent_two = standardize(view_two, average_two, inv_two)
    gathered_one = lax.all_gather(sent_one, "dp", axis=0, tiled=True)
    gathered_two = lax.all_gather(sent_two, "feat", axis=0, tiled=True)
    correlation = contract_rows(gathered_one, gathered_two) / batch_rows
    tile_rows, tile_cols = correlation.shape
    row_ids = lax.axis_index("feat") * tile_rows + lax.broadcasted_iota(
        jnp.int32, correlation.shape, 0
    )
    col_ids = lax.axis_index("dp") * tile_cols + lax.broadcasted_iota(
        jnp.int32, correlation.shape, 1
    )
    on_diagonal = row_ids == col_ids
    tile_loss = jnp.sum(
        jnp.where(
            on_diagonal,
            (1.0 - correlation) * (1.0 - correlation),
            off_weight * correlation * correlation,
        )
    )
    barlow = lax.psum(tile_loss, ("dp", "feat"))
    loss_value = jnp.reshape(barlow / F, (1,))
    gradient = (
        jnp.where(on_diagonal, -2.0 * (1.0 - correlation), 2.0 * off_weight * correlation)
        * loss_scale[0]
    ).astype(jnp.bfloat16)
    block = gathered_two
    upstream_one = (
        lax.psum_scatter(
            lax.dot_general(
                block, gradient, (((1,), (1,)), ((), ())), preferred_element_type=jnp.float32
            ),
            "dp",
            scatter_dimension=0,
            tiled=True,
        )
        / batch_rows
    )
    block = gathered_one
    upstream_two = (
        lax.psum_scatter(
            jnp.dot(block, gradient, preferred_element_type=jnp.float32),
            "feat",
            scatter_dimension=0,
            tiled=True,
        )
        / batch_rows
    )
    first_one = jnp.sum(upstream_one, axis=0)
    second_one = jnp.sum(upstream_one * sent_one.astype(jnp.float32), axis=0)
    first_one, second_one = lax.psum((first_one, second_one), "dp")
    first_two = jnp.sum(upstream_two, axis=0)
    second_two = jnp.sum(upstream_two * sent_two.astype(jnp.float32), axis=0)
    first_two, second_two = lax.psum((first_two, second_two), "feat")
    delta_one = apply_delta(upstream_one, sent_one, inv_one, first_one, second_one, batch_rows)
    delta_two = apply_delta(upstream_two, sent_two, inv_two, first_two, second_two, batch_rows)
    block = inputs_one
    weight_grad_one = contract_rows(block, lax.all_gather(delta_one, "dp", axis=0, tiled=True))
    block = inputs_two
    weight_grad_two = contract_rows(block, lax.all_gather(delta_two, "feat", axis=0, tiled=True))
    return (loss_value, weight_grad_one, weight_grad_two)


def solution(mesh):
    placed = (P("dp", "feat"), P("feat", "dp"), P(None, "dp"), P(None, "feat"), P())
    return jax.shard_map(
        per_device,
        mesh=mesh,
        in_specs=placed,
        out_specs=(P(), P("dp", "feat"), P("feat", "dp")),
        check_vma=False,
    )
```

profile of v0, /device:TPU:6, one launch (start us, length us, event | category | flops | bytes accessed | tf_op | source)
XLA Modules:
  0.0 654.4 jit_solution(1729741260805179228)
XLA Ops:
  7.2 0.0 all-gather.7.cloned.1.call-start
  7.2 1.0 convert_reduce_fusion
  8.2 45.1 %all-reduce.1 = (f32[512]{0:T(512)S(1)}, f32[512]{0:T(512)S(1)}) all-reduce(f32[512]{0:T(512)S(1)} %get-tuple-element.11, f32[512]{0:T(512)S(1)} %get-tuple-element.10), channel_id=1, replica_groups=mesh['dp'=16,'feat'=16] {'feat'}, use_global_device_ids=true, to_apply=%region_7.0 | all-reduce | flops 1024 | bytes 8192 | tf_op jit(solution)/shard_map/psum | solution.py:48
  53.4 1.7 fusion.17
  55.1 0.0 all-gather.7.cloned.1.call-update
  55.1 0.0 all-gather.5.cloned.1.call-start
  55.1 1.0 convert_reduce_fusion.1
  56.2 22.9 %all-reduce.3 = (f32[512]{0:T(512)S(1)}, f32[512]{0:T(512)S(1)}) all-reduce(f32[512]{0:T(512)S(1)} %get-tuple-element.13, f32[512]{0:T(512)S(1)} %get-tuple-element.12), channel_id=1, replica_groups=mesh['dp'=16,'feat'=16] {'dp'}, use_global_device_ids=true, to_apply=%region_3.0 | all-reduce | flops 1024 | bytes 8192 | tf_op jit(solution)/shard_map/psum | solution.py:45
  79.1 1.7 fusion.14
  80.8 0.0 all-gather.5.cloned.1.call-update
  80.8 0.0 reduce-scatter.5.cloned.1.call-start
  81.5 67.6 %all-gather.7.cloned.1.call-done = bf16[3840,512]{1,0:T(8,128)(2,1)} async-done(((bf16[240,512]{1,0:T(8,128)(2,1)}), bf16[3840,512]{1,0:T(8,128)(2,1)}) %all-gather.7.cloned.1.call-update) | async-done | bytes 3932176 | tf_op jit(solution)/shard_map/all_gather | solution.py:53
  149.1 37.6 %all-gather.5.cloned.1.call-done = bf16[3840,512]{1,0:T(8,128)(2,1)} async-done(((bf16[240,512]{1,0:T(8,128)(2,1)}), bf16[3840,512]{1,0:T(8,128)(2,1)}) %all-gather.5.cloned.1.call-update) | async-done | bytes 3932176 | tf_op jit(solution)/shard_map/all_gather | solution.py:52
  186.7 0.0 copy-start
  186.7 6.5 fusion
  193.2 0.0 copy-done
  193.2 5.6 fusion.19
  198.8 0.0 reduce-scatter.5.cloned.1.call-update
  198.8 0.0 reduce-scatter.3.cloned.1.call-start
  198.9 7.6 %fusion.21 = f32[3840,512]{1,0:T(8,128)} fusion(bf16[3840,512]{1,0:T(8,128)(2,1)} %all-gather.7.cloned.1.call-done, f32[512,512]{1,0:T(8,128)S(1)} %get-tuple-element.27, f32[]{:T(128)} %bitcast.14, s32[512]{0:T(512)S(1)} %get-tuple-element.28, s32[512]{0:T(512)S(1)} %get-tuple-element.29), kind=kOutput, calls=%fused_computation.44 | convolution fusion | flops 2015363072 | bytes 12849156 | tf_op jit(solution)/shard_map/dot_general | solution.py:79
  206.5 0.0 copy-start.1
  206.5 0.0 copy-start.2
  206.5 0.0 reduce-scatter.3.cloned.1.call-update
  206.5 0.0 all-gather.11.cloned.1.call-start
  206.5 218.4 %reduce-scatter.5.cloned.1.call-done = f32[240,512]{1,0:T(8,128)} async-done(((f32[3840,512]{1,0:T(8,128)}), f32[240,512]{1,0:T(8,128)}) %reduce-scatter.5.cloned.1.call-update) | async-done | bytes 491536 | tf_op jit(solution)/shard_map/reduce_scatter | solution.py:90
  425.0 0.0 copy-done.1
  425.0 1.2 multiply_reduce_fusion
  426.2 38.9 %all-reduce = (f32[512]{0:T(512)S(1)}, f32[512]{0:T(512)S(1)}) all-reduce(f32[512]{0:T(512)S(1)} %get-tuple-element.7, f32[512]{0:T(512)S(1)} %get-tuple-element.6), channel_id=1, replica_groups=mesh['dp'=16,'feat'=16] {'feat'}, use_global_device_ids=true, to_apply=%region_19.20 | all-reduce | flops 1024 | bytes 8192 | tf_op jit(solution)/shard_map/psum | solution.py:103
  465.0 1.9 fusion.12
  466.9 0.0 all-gather.11.cloned.1.call-update
  466.9 0.0 all-gather.9.cloned.1.call-start
  467.0 30.6 %reduce-scatter.3.cloned.1.call-done = f32[240,512]{1,0:T(8,128)} async-done(((f32[3840,512]{1,0:T(8,128)}), f32[240,512]{1,0:T(8,128)}) %reduce-scatter.3.cloned.1.call-update) | async-done | bytes 491536 | tf_op jit(solution)/shard_map/reduce_scatter | solution.py:78
  497.5 0.0 copy-done.2
  497.6 1.2 multiply_reduce_fusion.1
  498.7 27.3 %all-reduce.2 = (f32[512]{0:T(512)S(1)}, f32[512]{0:T(512)S(1)}) all-reduce(f32[512]{0:T(512)S(1)} %get-tuple-element.9, f32[512]{0:T(512)S(1)} %get-tuple-element.8), channel_id=1, replica_groups=mesh['dp'=16,'feat'=16] {'dp'}, use_global_device_ids=true, to_apply=%region_14.15 | all-reduce | flops 1024 | bytes 8192 | tf_op jit(solution)/shard_map/psum | solution.py:100
  526.0 1.9 fusion.7
  527.9 0.0 all-gather.9.cloned.1.call-update
  527.9 80.9 %psum.67 = f32[]{:T(128)} all-reduce(f32[]{:T(128)} %get-tuple-element.26), channel_id=1, replica_groups=mesh['dp'=16,'feat'=16] {'dp','feat'}, use_global_device_ids=true, to_apply=%region_9.10 | all-reduce | flops 1 | bytes 8 | tf_op jit(solution)/shard_map/psum | solution.py:70
  609.5 0.0 all-gather.11.cloned.1.call-done
  609.5 5.5 convolution_bitcast_fusion
  615.0 1.3 copy.9
  616.3 23.3 %all-gather.9.cloned.1.call-done = bf16[3840,512]{1,0:T(8,128)(2,1)} async-done(((bf16[240,512]{1,0:T(8,128)(2,1)}), bf16[3840,512]{1,0:T(8,128)(2,1)}) %all-gather.9.cloned.1.call-update) | async-done | bytes 3932176 | tf_op jit(solution)/shard_map/all_gather | solution.py:107
  639.6 5.5 convolution_bitcast_fusion.1
  645.1 1.3 copy.8
  (5 shorter events, 0.0 us)
Async XLA Ops:
  7.2 141.9 %all-gather.7.cloned.1.call-start = ((), (), s32[]{:S(2)}) async-start(), calls=%async_computation.3 | async-start | bytes 4177920 | tf_op jit(solution)/shard_map/all_gather | solution.py:53
  55.1 131.6 %all-gather.5.cloned.1.call-start = ((), (), s32[]{:S(2)}) async-start(), calls=%async_computation.2 | async-start | bytes 4177920 | tf_op jit(solution)/shard_map/all_gather | solution.py:52
  80.8 344.2 %reduce-scatter.5.cloned.1.call-start = ((), (), s32[]{:S(2)}) async-start(), calls=%async_computation.6 | async-start | bytes 8355840 | tf_op jit(solution)/shard_map/reduce_scatter | solution.py:90
  186.7 6.5 copy-start
  198.8 298.7 %reduce-scatter.3.cloned.1.call-start = ((), (), s32[]{:S(2)}) async-start(), calls=%async_computation.4 | async-start | bytes 8355840 | tf_op jit(solution)/shard_map/reduce_scatter | solution.py:78
  206.5 218.5 %copy-start.1 = (bf16[240,512]{1,0:T(8,128)(2,1)S(1)}, bf16[240,512]{1,0:T(8,128)(2,1)}, u32[]{:S(2)}) copy-start(bf16[240,512]{1,0:T(8,128)(2,1)} %param.6) | copy-start | bytes 737284
  206.5 291.1 %copy-start.2 = (bf16[240,512]{1,0:T(8,128)(2,1)S(1)}, bf16[240,512]{1,0:T(8,128)(2,1)}, u32[]{:S(2)}) copy-start(bf16[240,512]{1,0:T(8,128)(2,1)} %param.5) | copy-start | bytes 737284
  206.5 403.0 %all-gather.11.cloned.1.call-start = ((), (), s32[]{:S(2)}) async-start(), calls=%async_computation.7 | async-start | bytes 4177920 | tf_op jit(solution)/shard_map/all_gather | solution.py:109
  466.9 172.7 %all-gather.9.cloned.1.call-start = ((), (), s32[]{:S(2)}) async-start(), calls=%async_computation.5 | async-start | bytes 4177920 | tf_op jit(solution)/shard_map/all_gather | solution.py:107
Sparse Core Ops, SparseCore 0:
  55.2 93.8 all-gather.6
  151.5 35.1 all-gather.4
  198.9 226.0 reduce-scatter.4
  427.4 70.0 reduce-scatter.2
  500.6 101.4 all-gather.10
  604.3 35.2 all-gather.8
where the time goes:
time: 657 us; the launch traced here: 654 us
  waiting for transfers between devices  378 us (58%)
  blocking collectives  215 us (33%)
  matrix products  30.7 us (5%)
  between operations  16.6 us (3%)
  other arithmetic  11.6 us (2%)
    reduce_scatter x1, waiting for transfers between devices, per_device(): lax.psum_scatter(jnp.dot(block, gradient, preferred_element_type=jnp.floa...  218 us
    psum x1, blocking collectives, per_device(): barlow = lax.psum(tile_loss, ('dp', 'feat'))  80.9 us
    all_gather x1, waiting for transfers between devices, per_device(): gathered_two = lax.all_gather(sent_two, 'feat', axis=0, tiled=True)  67.6 us
    psum x1, blocking collectives, per_device(): sums_two, squares_two = lax.psum((sums_two, squares_two), 'feat')  45.1 us
    psum x1, blocking collectives, per_device(): first_two, second_two = lax.psum((first_two, second_two), 'feat')  38.9 us
    all_gather x1, waiting for transfers between devices, per_device(): gathered_one = lax.all_gather(sent_one, 'dp', axis=0, tiled=True)  37.6 us
    reduce_scatter x1, waiting for transfers between devices, per_device(): lax.psum_scatter(lax.dot_general(block, gradient, (((1,), (1,)), ((), ())...  30.6 us
    psum x1, blocking collectives, per_device(): first_one, second_one = lax.psum((first_one, second_one), 'dp')  27.3 us
  transfers between devices with their start and end apart: 6, of which 5 were waited for; matrix products, arithmetic and copies ran while one was open for 4% of the time, Pallas kernels for 0%

commit v1 on v0

v1 whole, which is shorter than its diff:
```python
import jax
import jax.numpy as jnp
from jax import lax
from jax.experimental import pallas as pl
from jax.experimental.pallas import tpu as pltpu
from jax.sharding import PartitionSpec as P

F = 8192
off_weight = 0.0051
epsilon = 1e-05
MESH = pl.DeviceIdType.MESH
f32 = jnp.float32
bf16 = jnp.bfloat16

NX = 4
NZ = 8
SIGN = {"zp": 1, "zm": -1, "xp": 1, "xm": -1}
KZ = {("zp", 0): 4, ("zm", 0): 3, ("zp", 1): 3, ("zm", 1): 4}
KX = {("xp", 0): 2, ("xm", 0): 1, ("xp", 1): 1, ("xm", 1): 2}
ZSLOT = {}
for key, hops in KZ.items():
    for hop in range(hops):
        ZSLOT[key + (hop,)] = len(ZSLOT)
XSLOT = {}
for key, hops in KX.items():
    for hop in range(hops):
        XSLOT[key + (hop,)] = len(XSLOT)
CORDER = [(0, 2), (1, 2), (1, 1), (0, 3), (0, 1), (1, 3), (1, 0), (0, 0)]
CSLOT = {key: n for n, key in enumerate(CORDER)}
NSEM = 112


def dot_tn(left, right):
    return lax.dot_general(left, right, (((0,), (0,)), ((), ())), preferred_element_type=f32)


def dot_nt(left, right):
    return lax.dot_general(left, right, (((1,), (1,)), ((), ())), preferred_element_type=f32)


def dot_nn(left, right):
    return lax.dot_general(left, right, (((1,), (0,)), ((), ())), preferred_element_type=f32)


def fold8(block):
    total = block[0:8]
    for k in range(8, block.shape[0], 8):
        total = total + block[k : k + 8]
    return total


def kernel(
    view1, view2, in1, in2, scale_ref,
    loss_ref, w1_ref, w2_ref,
    V1, V2, D1, D2, X1, X2,
    zs, zr, cs, cr, xs, xr, ys, yr, U1, U2,
    C, G, GH, GL, M1, M2, A1, R1, A2, R2, AL, RL,
    ssem, rsem, lsem,
):
    R = view1.shape[0]
    B = V1.shape[0]
    T = V1.shape[1]
    dp = lax.axis_index("dp")
    ft = lax.axis_index("feat")
    c = lax.rem(dp, 2)
    x = lax.rem(lax.div(dp, 2), NX)
    yl = lax.div(dp, 2 * NX)
    yh = lax.rem(ft, 2)
    z = lax.div(ft, 2)

    def dpi(r, dx, other=0):
        y_ = yl if r == 0 else 1 - yl
        c_ = 1 - c if other else c
        return (y_ * NX + lax.rem(x + (dx % NX), NX)) * 2 + c_

    def fti(r, dz):
        y_ = yh if r == 0 else 1 - yh
        return lax.rem(z + (dz % NZ), NZ) * 2 + y_

    def rows(i):
        return pl.ds(pl.multiple_of(i * R, 16), R)

    def at(buf, i):
        return buf.at[rows(i)]

    to_core = {"dp": dpi(0, 0, 1), "feat": ft}
    to_yl = {"dp": dpi(1, 0), "feat": ft}
    to_yh = {"dp": dp, "feat": fti(1, 0)}
    to = {
        "xp": {"dp": dpi(0, 1), "feat": ft},
        "xm": {"dp": dpi(0, -1), "feat": ft},
        "zp": {"dp": dp, "feat": fti(0, 1)},
        "zm": {"dp": dp, "feat": fti(0, -1)},
    }
    xa = x + 1 - 2 * lax.rem(x, 2)
    xb = NX - 1 - x
    za = z + 1 - 2 * lax.rem(z, 2)
    zb = z + 2 - 4 * lax.rem(lax.div(z, 2), 2)
    dp_steps = [
        to_core,
        to_yl,
        {"dp": (yl * NX + xa) * 2 + c, "feat": ft},
        {"dp": (yl * NX + xb) * 2 + c, "feat": ft},
    ]
    to_zb = {"dp": dp, "feat": zb * 2 + yh}
    to_zc = {"dp": dp, "feat": fti(0, 4)}
    feat_steps = [to_yh, {"dp": dp, "feat": za * 2 + yh}, to_zb, to_zc]

    peers = [to_core, to_yl, to_yh, to["xp"], to["xm"], to["zp"], to["zm"], to_zb, to_zc]
    barrier = pltpu.get_barrier_semaphore()
    for peer in peers:
        pl.semaphore_signal(barrier, inc=1, device_id=peer, device_id_type=MESH)
    local = [
        pltpu.make_async_copy(view1, at(V1, dp), lsem.at[0]),
        pltpu.make_async_copy(view2, at(V2, ft), lsem.at[1]),
        pltpu.make_async_copy(in1, X1, lsem.at[2]),
        pltpu.make_async_copy(in2, X2, lsem.at[3]),
    ]
    for copy in local:
        copy.start()
    pl.semaphore_wait(barrier, len(peers))

    names = {}
    flying = {}

    def index(name):
        return names.setdefault(name, len(names))

    def send(name, src, dst, dev):
        k = index(name)
        copy = pltpu.make_async_remote_copy(
            src_ref=src, dst_ref=dst, send_sem=ssem.at[k], recv_sem=rsem.at[k],
            device_id=dev, device_id_type=MESH,
        )
        copy.start()
        flying[name] = copy

    def recv(name, dst):
        k = index(name)
        pltpu.make_async_remote_copy(
            src_ref=dst, dst_ref=dst, send_sem=ssem.at[k], recv_sem=rsem.at[k],
            device_id=to_core, device_id_type=MESH,
        ).wait_recv()

    def drain(keep=lambda name: True):
        for name in [n for n in flying if keep(n)]:
            flying.pop(name).wait_send()

    def start_a(tag, A, src):
        own = at(A, dp)
        send((tag, "yl"), src, own, to_yl)
        send((tag, "xp", 0, 1), src, own, to["xp"])
        send((tag, "xm", 0, 1), src, own, to["xm"])
        send((tag, "c", 0, 0), src, own, to_core)

    def start_b(tag, Bb, src):
        own = at(Bb, ft)
        send((tag, "yh"), src, own, to_yh)
        send((tag, "zp", 0, 1), src, own, to["zp"])
        send((tag, "zm", 0, 1), src, own, to["zm"])

    def ev_yl(tag, A):
        i = dpi(1, 0)
        recv((tag, "yl"), at(A, i))
        send((tag, "xp", 1, 1), at(A, i), at(A, i), to["xp"])
        send((tag, "xm", 1, 1), at(A, i), at(A, i), to["xm"])
        send((tag, "c", 1, 0), at(A, i), at(A, i), to_core)
        return i

    def ev_yh(tag, Bb):
        i = fti(1, 0)
        recv((tag, "yh"), at(Bb, i))
        send((tag, "zp", 1, 1), at(Bb, i), at(Bb, i), to["zp"])
        send((tag, "zm", 1, 1), at(Bb, i), at(Bb, i), to["zm"])
        return i

    def ev_x(tag, A, d, r, h):
        dx = (-SIGN[d] * h) % NX
        i = dpi(r, dx)
        recv((tag, d, r, h), at(A, i))
        if h < KX[d, r]:
            send((tag, d, r, h + 1), at(A, i), at(A, i), to[d])
        send((tag, "c", r, dx), at(A, i), at(A, i), to_core)
        return i

    def ev_z(tag, Bb, d, r, h):
        i = fti(r, -SIGN[d] * h)
        recv((tag, d, r, h), at(Bb, i))
        if h < KZ[d, r]:
            send((tag, d, r, h + 1), at(Bb, i), at(Bb, i), to[d])
        return i

    def ev_c(tag, A, r, dx):
        i = dpi(r, dx, 1)
        recv((tag, "c", r, dx), at(A, i))
        return i

    CH = 48

    def moments(V, M, i):
        base = i * R

        def body(k, carry):
            s, q = carry
            v = V[pl.ds(pl.multiple_of(base + k * CH, 16), CH), :].astype(f32)
            return s + fold8(v), q + fold8(v * v)

        s, q = lax.fori_loop(0, R // CH, body, (M[0:8, :], M[8:16, :]))
        M[0:8, :] = s
        M[8:16, :] = q

    def normalize(V, M):
        average = jnp.sum(M[0:8, :], axis=0, keepdims=True) / B
        spread = jnp.sum(M[8:16, :], axis=0, keepdims=True) / B - average * average
        inv = lax.rsqrt(spread + epsilon)
        M[16:24, :] = jnp.broadcast_to(inv, (8, T))

        def body(k, total):
            at_ = pl.ds(pl.multiple_of(k * CH, 16), CH)
            n = ((V[at_, :].astype(f32) - average) * inv).astype(bf16)
            V[at_, :] = n
            return total + fold8(n.astype(f32))

        total = lax.fori_loop(0, B // CH, body, jnp.zeros((8, T), f32))
        M[24:32, :] = jnp.broadcast_to(jnp.sum(total, axis=0, keepdims=True), (8, T))

    M1[...] = jnp.zeros_like(M1)
    M2[...] = jnp.zeros_like(M2)
    start_b("g", V2, view2)
    start_a("g", V1, view1)
    local[0].wait()
    local[1].wait()
    moments(V1, M1, dp)
    moments(V2, M2, ft)

    def gz(d, r, h):
        moments(V2, M2, ev_z("g", V2, d, r, h))

    def gx(d, r, h):
        moments(V1, M1, ev_x("g", V1, d, r, h))

    def gc(r, dx):
        moments(V1, M1, ev_c("g", V1, r, dx))

    gz("zp", 0, 1)
    gz("zm", 0, 1)
    moments(V1, M1, ev_yl("g", V1))
    gx("xp", 0, 1)
    gx("xm", 0, 1)
    moments(V2, M2, ev_yh("g", V2))
    gz("zp", 0, 2)
    gz("zm", 0, 2)
    gx("xp", 1, 1)
    gx("xm", 1, 1)
    gz("zp", 1, 1)
    gz("zm", 1, 1)
    gx("xp", 0, 2)
    gx("xm", 1, 2)
    gz("zp", 0, 3)
    gz("zm", 0, 3)
    gz("zp", 1, 2)
    gz("zm", 1, 2)
    for r, dx in CORDER:
        gc(r, dx)
    gz("zp", 0, 4)
    gz("zp", 1, 3)
    gz("zm", 1, 3)
    drain(lambda n: n[1] in ("c", "xp", "xm", "yl"))
    normalize(V1, M1)
    gz("zm", 1, 4)
    drain()
    normalize(V2, M2)

    KC = 768
    C[...] = dot_tn(V1[0:KC, :], V2[0:KC, :])

    def corr(k, carry):
        at_ = pl.ds(pl.multiple_of(k * KC, 16), KC)
        C[...] += dot_tn(V1[at_, :], V2[at_, :])
        return carry

    lax.fori_loop(1, B // KC, corr, 0)

    CG = 32
    scale = scale_ref[0]
    row0 = ft * T
    col0 = dp * T

    def grad(k, loss):
        at_ = pl.ds(pl.multiple_of(k * CG, CG), CG)
        corr_ = C[at_, :] / B
        row_ids = row0 + k * CG + lax.broadcasted_iota(jnp.int32, (CG, T), 0)
        col_ids = col0 + lax.broadcasted_iota(jnp.int32, (CG, T), 1)
        on = row_ids == col_ids
        miss = 1.0 - corr_
        loss = loss + fold8(jnp.where(on, miss * miss, off_weight * corr_ * corr_))
        g = (jnp.where(on, -2.0 * miss, 2.0 * off_weight * corr_) * scale).astype(bf16)
        G[at_, :] = g
        prod = g.astype(f32) * corr_
        high = prod.astype(bf16)
        GH[at_, :] = high
        GL[at_, :] = (prod - high.astype(f32)).astype(bf16)
        return loss

    loss = lax.fori_loop(0, T // CG, grad, jnp.zeros((8, T), f32))
    loss_tile = loss[:, 0:128]
    for k in range(128, T, 128):
        loss_tile = loss_tile + loss[:, k : k + 128]

    def p2(i):
        return dot_nn(V1[rows(i), :], G[...])

    def p1(i):
        return dot_nt(V2[rows(i), :], G[...])

    def zc(d, r, s):
        i = fti(r, SIGN[d] * (KZ[d, r] - s))
        val = p2(i)
        if s:
            prev = ZSLOT[d, r, s - 1]
            recv(("s", d, r, s - 1), zr.at[prev])
            val = val + zr[prev].astype(f32)
        slot = ZSLOT[d, r, s]
        zs[slot] = val.astype(bf16)
        send(("s", d, r, s), zs.at[slot], zr.at[slot], to[d])

    def z_end(r):
        val = p2(fti(r, 0))
        for d in ("zp", "zm"):
            last = KZ[d, r] - 1
            slot = ZSLOT[d, r, last]
            recv(("s", d, r, last), zr.at[slot])
            val = val + zr[slot].astype(f32)
        return val

    def core_send(r, dx):
        slot = CSLOT[r, dx]
        cs[slot] = p1(dpi(r, dx, 1)).astype(bf16)
        send(("s", "c", r, dx), cs.at[slot], cr.at[slot], to_core)

    def both(r, dx):
        dx = dx % NX
        val = p1(dpi(r, dx))
        slot = CSLOT[r, dx]
        recv(("s", "c", r, dx), cr.at[slot])
        return val + cr[slot].astype(f32)

    def xc(d, r, s):
        val = both(r, SIGN[d] * (KX[d, r] - s))
        if s:
            prev = XSLOT[d, r, s - 1]
            recv(("s", d, r, s - 1), xr.at[prev])
            val = val + xr[prev].astype(f32)
        slot = XSLOT[d, r, s]
        xs[slot] = val.astype(bf16)
        send(("s", d, r, s), xs.at[slot], xr.at[slot], to[d])

    def x_end(r):
        val = both(r, 0)
        for d in ("xp", "xm"):
            last = KX[d, r] - 1
            slot = XSLOT[d, r, last]
            recv(("s", d, r, last), xr.at[slot])
            val = val + xr[slot].astype(f32)
        return val

    zc("zp", 0, 0)
    zc("zm", 1, 0)
    zc("zp", 1, 0)
    zc("zm", 0, 0)
    for r, dx in CORDER:
        core_send(r, dx)

    ones = jnp.ones((16, T), bf16)
    second1 = dot_nt(ones, GH[...]) + dot_nt(ones, GL[...])
    second2 = dot_nn(ones, GH[...]) + dot_nn(ones, GL[...])
    lane_row = lax.broadcasted_iota(jnp.int32, (16, T), 0)

    def split_rows(M):
        s = jnp.concatenate([M[24:32, :], M[24:32, :]], axis=0)
        high = s.astype(bf16).astype(f32)
        low = s - high
        return jnp.where(lane_row == 0, high, jnp.where(lane_row == 1, low, 0.0)).astype(bf16)

    first1 = jnp.sum(dot_nt(split_rows(M2), G[...]), axis=0, keepdims=True) / B
    first2 = jnp.sum(dot_nn(split_rows(M1), G[...]), axis=0, keepdims=True) / B
    top = lane_row[0:8] == 0
    A1[0, :, 0:T] = jnp.where(top, jnp.broadcast_to(first1, (8, T)), second1[0:8])
    A1[0, :, T : T + 128] = loss_tile
    A2[0] = jnp.where(top, jnp.broadcast_to(first2, (8, T)), second2[0:8])

    def put(n):
        send(("a1", n), A1.at[n], R1.at[n], dp_steps[n])
        send(("a2", n), A2.at[n], R2.at[n], feat_steps[n])

    def take(n):
        recv(("a1", n), R1.at[n])
        recv(("a2", n), R2.at[n])
        A1[n + 1] = A1[n] + R1[n]
        A2[n + 1] = A2[n] + R2[n]

    put(0)
    xc("xp", 0, 0)
    xc("xm", 1, 0)
    zc("zp", 0, 1)
    zc("zm", 1, 1)
    take(0)
    put(1)
    xc("xp", 1, 0)
    xc("xm", 0, 0)
    zc("zp", 1, 1)
    zc("zm", 0, 1)
    take(1)
    put(2)
    xc("xp", 0, 1)
    xc("xm", 1, 1)
    zc("zp", 0, 2)
    zc("zm", 1, 2)
    take(2)
    put(3)
    ys[0] = x_end(1).astype(bf16)
    send(("s", "yl"), ys.at[0], yr.at[0], to_yl)
    zc("zp", 1, 2)
    zc("zm", 0, 2)
    take(3)

    def delta(U, V, M, A, D, i):
        stats = A[4]
        first = stats[0:1, 0:T] / B
        second = stats[1:2, 0:T] / B
        inv = M[16:17, :]

        def body(k, carry):
            off = pl.multiple_of(k * CH, 16)
            at_ = pl.ds(pl.multiple_of(i * R + k * CH, 16), CH)
            own = V[at_, :].astype(f32)
            D[at_, :] = (inv * (U[pl.ds(off, CH), :] / B - first - own * second)).astype(bf16)
            return carry

        lax.fori_loop(0, R // CH, body, 0)

    val = x_end(0)
    recv(("s", "yl"), yr.at[0])
    U1[...] = val + yr[0].astype(f32)
    delta(U1, V1, M1, A1, D1, dp)
    start_a("d", D1, at(D1, dp))
    zc("zp", 0, 3)
    zc("zm", 1, 3)

    AL[0] = A1[4, :, T : T + 128]

    def put_l(n):
        send(("al", n), AL.at[n], RL.at[n], feat_steps[n])

    def take_l(n):
        recv(("al", n), RL.at[n])
        AL[n + 1] = AL[n] + RL[n]

    put_l(0)
    ys[1] = z_end(1).astype(bf16)
    send(("s", "yh"), ys.at[1], yr.at[1], to_yh)
    ev_yl("d", D1)
    ev_x("d", D1, "xp", 0, 1)
    ev_x("d", D1, "xm", 0, 1)
    take_l(0)
    put_l(1)
    val = z_end(0)
    recv(("s", "yh"), yr.at[1])
    U2[...] = val + yr[1].astype(f32)
    delta(U2, V2, M2, A2, D2, ft)
    start_b("d", D2, at(D2, ft))

    ev_x("d", D1, "xp", 1, 1)
    ev_x("d", D1, "xm", 1, 1)
    ev_x("d", D1, "xp", 0, 2)
    ev_x("d", D1, "xm", 1, 2)
    take_l(1)
    put_l(2)
    ev_z("d", D2, "zp", 0, 1)
    ev_z("d", D2, "zm", 0, 1)
    take_l(2)
    put_l(3)
    ev_yh("d", D2)
    ev_z("d", D2, "zp", 0, 2)
    ev_z("d", D2, "zm", 0, 2)
    take_l(3)
    loss_ref[0] = jnp.sum(AL[4]) / F
    for r, dx in CORDER:
        ev_c("d", D1, r, dx)
    local[2].wait()
    local[3].wait()

    def weights(w_ref, X, D):
        w_ref[...] = dot_tn(X[0:KC, :], D[0:KC, :])

        def body(k, carry):
            at_ = pl.ds(pl.multiple_of(k * KC, 16), KC)
            w_ref[...] += dot_tn(X[at_, :], D[at_, :])
            return carry

        lax.fori_loop(1, B // KC, body, 0)

    ev_z("d", D2, "zp", 1, 1)
    ev_z("d", D2, "zm", 1, 1)
    ev_z("d", D2, "zp", 0, 3)
    ev_z("d", D2, "zm", 0, 3)
    weights(w1_ref, X1, D1)
    ev_z("d", D2, "zp", 1, 2)
    ev_z("d", D2, "zm", 1, 2)
    ev_z("d", D2, "zp", 0, 4)
    ev_z("d", D2, "zp", 1, 3)
    ev_z("d", D2, "zm", 1, 3)
    ev_z("d", D2, "zm", 1, 4)
    weights(w2_ref, X2, D2)
    drain()
    assert len(names) <= NSEM


def per_device(view_one, view_two, inputs_one, inputs_two, loss_scale):
    R, T = view_one.shape
    B = inputs_one.shape[0]
    block = (R, T)
    anywhere = pl.BlockSpec(memory_space=pl.ANY)
    vmem = pl.BlockSpec(memory_space=pltpu.VMEM)
    smem = pl.BlockSpec(memory_space=pltpu.SMEM)
    V = pltpu.VMEM
    scratch = [
        V((B, T), bf16), V((B, T), bf16), V((B, T), bf16), V((B, T), bf16),
        V((B, T), bf16), V((B, T), bf16),
        V((len(ZSLOT),) + block, bf16), V((len(ZSLOT),) + block, bf16),
        V((len(CSLOT),) + block, bf16), V((len(CSLOT),) + block, bf16),
        V((len(XSLOT),) + block, bf16), V((len(XSLOT),) + block, bf16),
        V((2,) + block, bf16), V((2,) + block, bf16),
        V(block, f32), V(block, f32),
        V((T, T), f32), V((T, T), bf16), V((T, T), bf16), V((T, T), bf16),
        V((32, T), f32), V((32, T), f32),
        V((5, 8, T + 128), f32), V((4, 8, T + 128), f32),
        V((5, 8, T), f32), V((4, 8, T), f32),
        V((5, 8, 128), f32), V((4, 8, 128), f32),
        pltpu.SemaphoreType.DMA((NSEM,)),
        pltpu.SemaphoreType.DMA((NSEM,)),
        pltpu.SemaphoreType.DMA((4,)),
    ]
    return pl.pallas_call(
        kernel,
        out_shape=(
            jax.ShapeDtypeStruct((1,), f32),
            jax.ShapeDtypeStruct((T, T), f32),
            jax.ShapeDtypeStruct((T, T), f32),
        ),
        in_specs=[anywhere] * 4 + [smem],
        out_specs=(smem, vmem, vmem),
        scratch_shapes=scratch,
        compiler_params=pltpu.CompilerParams(
            collective_id=0, has_side_effects=True, vmem_limit_bytes=58 * 1024 * 1024
        ),
        cost_estimate=pl.CostEstimate(
            flops=10 * B * T * T, bytes_accessed=4 * B * T + 8 * T * T, transcendentals=0
        ),
    )(view_one, view_two, inputs_one, inputs_two, loss_scale)


def solution(mesh):
    placed = (P("dp", "feat"), P("feat", "dp"), P(None, "dp"), P(None, "feat"), P())
    return jax.shard_map(
        per_device,
        mesh=mesh,
        in_specs=placed,
        out_specs=(P(), P("dp", "feat"), P("feat", "dp")),
        check_vma=False,
    )
```

time: 657 us -> 165 us (0.25)
  waiting for transfers between devices: 378 us -> 0 us
  blocking collectives: 215 us -> 0 us
  Pallas kernels: 0 us -> 156 us
  matrix products: 30.7 us -> 0 us
  between operations: 16.6 us -> 3.02 us
  other arithmetic: 11.6 us -> 0 us
    reduce_scatter x2 -> x0, waiting for transfers between devices: 249 us -> none  [the longest x1 218 us: per_device(): lax.psum_scatter(jnp.dot(block, gradient, preferred_element_type=jnp.floa...]
    psum x5 -> x0, blocking collectives: 215 us -> none  [the longest x1 80.9 us: per_device(): barlow = lax.psum(tile_loss, ('dp', 'feat'))]
    pallas_call x0 -> x1, Pallas kernels: none -> 156 us  [per_device(): pl.pallas_call(kernel, out_shape=(jax.ShapeDtypeStruct((1,), f32), jax.Sh...]
    all_gather x4 -> x0, waiting for transfers between devices: 129 us -> none  [the longest x1 67.6 us: per_device(): gathered_two = lax.all_gather(sent_two, 'feat', axis=0, tiled=True)]
    dot_general x5 -> x0, matrix products: 30.7 us -> none  [the longest x3 17.5 us: contract_rows(): lax.dot_general(left, right, (((0,), (0,)), ((), ())), preferred_element_...]
    convert_element_type x4 -> x0, other arithmetic: 7.16 us -> none  [the longest x2 3.76 us: apply_delta(): (inv_std * (upstream - first / batch_rows - own * second / batch_rows)).a...]
  transfers between devices with their start and end apart: 6 -> 0, of which waited for: 5 -> 0; matrix products, arithmetic and copies ran while one was open for 4% -> 0% of each run, Pallas kernels for 0% -> 0%
where the time goes in v1:
time: 165 us; the launch traced here: 164 us
  Pallas kernels  156 us (95%)
  local copies, waits for them, and re-layouts  4.52 us (3%)
  between operations  3.02 us (2%)
    pallas_call x1, Pallas kernels, per_device(): pl.pallas_call(kernel, out_shape=(jax.ShapeDtypeStruct((1,), f32), jax.Sh...  156 us
    unnamed x2, local copies, waits for them, and re-layouts  4.52 us

profile of v1, /device:TPU:6, one launch (start us, length us, event | category | flops | bytes accessed | tf_op | source)
XLA Modules:
  0.0 163.8 jit_solution(4568071812782427412)
XLA Ops:
  1.3 156.3 %shard_map.76 = (f32[1]{0:T(128)}, f32[512,512]{1,0:T(8,128)}, f32[512,512]{1,0:T(8,128)}) custom-call(bf16[240,512]{1,0:T(8,128)(2,1)} %view1.1, bf16[240,512]{1,0:T(8,128)(2,1)} %view2.1, bf16[3840,512]{1,0:T(8,128)(2,1)} %in1.1, bf16[3840,512]{1,0:T(8,128)(2,1)} %in2.1, f32[1]{0:T(128)S(6)} %copy.11.scale_ref), custom_call_target="tpu_custom_call" | custom-call | flops 10066329600 | bytes 9961472 | tf_op jit(solution)/shard_map/pallas_call | solution.py:544
  158.2 2.3 %copy.13 = f32[512,512]{1,0:T(8,128)} copy(f32[512,512]{1,0:T(8,128)} %get-tuple-element.7) | data formatting | bytes 2097152
  160.4 2.3 %copy.14 = f32[512,512]{1,0:T(8,128)} copy(f32[512,512]{1,0:T(8,128)} %get-tuple-element.8) | data formatting | bytes 2097152

commit v2 on v1

--- a/solution.py
+++ b/solution.py
@@ -14,20 +14,23 @@
 
 NX = 4
 NZ = 8
-SIGN = {"zp": 1, "zm": -1, "xp": 1, "xm": -1}
-KZ = {("zp", 0): 4, ("zm", 0): 3, ("zp", 1): 3, ("zm", 1): 4}
+SIGN = {"xp": 1, "xm": -1}
 KX = {("xp", 0): 2, ("xm", 0): 1, ("xp", 1): 1, ("xm", 1): 2}
-ZSLOT = {}
-for key, hops in KZ.items():
-    for hop in range(hops):
-        ZSLOT[key + (hop,)] = len(ZSLOT)
+PIECES = ((0, 128), (128, 112))
+ZSLOT = {
+    key: n
+    for n, key in enumerate(
+        [(1, 4), (1, 3), (1, -3), (1, -2), (0, 4), (0, 3), (0, 2), (0, 1), (0, -3), (0, -2), (0, -1)]
+        + [("y", 2), ("y", -1), ("y", 1), ("y", 0)]
+    )
+}
 XSLOT = {}
 for key, hops in KX.items():
     for hop in range(hops):
         XSLOT[key + (hop,)] = len(XSLOT)
 CORDER = [(0, 2), (1, 2), (1, 1), (0, 3), (0, 1), (1, 3), (1, 0), (0, 0)]
 CSLOT = {key: n for n, key in enumerate(CORDER)}
-NSEM = 112
+NSEM = 200
 
 
 def dot_tn(left, right):
@@ -73,15 +76,22 @@
         c_ = 1 - c if other else c
         return (y_ * NX + lax.rem(x + (dx % NX), NX)) * 2 + c_
 
+    turn = 1 - 2 * c
+
     def fti(r, dz):
         y_ = yh if r == 0 else 1 - yh
-        return lax.rem(z + (dz % NZ), NZ) * 2 + y_
+        return lax.rem(z + NZ + dz * turn, NZ) * 2 + y_
 
     def rows(i):
         return pl.ds(pl.multiple_of(i * R, 16), R)
 
-    def at(buf, i):
-        return buf.at[rows(i)]
+    def at(buf, i, u=None):
+        if u is None:
+            return buf.at[rows(i)]
+        return buf.at[pl.ds(pl.multiple_of(i * R + PIECES[u][0], 16), PIECES[u][1])]
+
+    def part(buf, slot, u):
+        return buf.at[slot, pl.ds(*PIECES[u])]
 
     to_core = {"dp": dpi(0, 0, 1), "feat": ft}
     to_yl = {"dp": dpi(1, 0), "feat": ft}
@@ -89,8 +99,8 @@
     to = {
         "xp": {"dp": dpi(0, 1), "feat": ft},
         "xm": {"dp": dpi(0, -1), "feat": ft},
-        "zp": {"dp": dp, "feat": fti(0, 1)},
-        "zm": {"dp": dp, "feat": fti(0, -1)},
+        "p": {"dp": dp, "feat": fti(0, 1)},
+        "m": {"dp": dp, "feat": fti(0, -1)},
     }
     xa = x + 1 - 2 * lax.rem(x, 2)
     xb = NX - 1 - x
@@ -106,7 +116,7 @@
     to_zc = {"dp": dp, "feat": fti(0, 4)}
     feat_steps = [to_yh, {"dp": dp, "feat": za * 2 + yh}, to_zb, to_zc]
 
-    peers = [to_core, to_yl, to_yh, to["xp"], to["xm"], to["zp"], to["zm"], to_zb, to_zc]
+    peers = [to_core, to_yl, to_yh, to["xp"], to["xm"], to["p"], to["m"], to_zb, to_zc]
     barrier = pltpu.get_barrier_semaphore()
     for peer in peers:
         pl.semaphore_signal(barrier, inc=1, device_id=peer, device_id_type=MESH)
@@ -155,9 +165,11 @@
 
     def start_b(tag, Bb, src):
         own = at(Bb, ft)
-        send((tag, "yh"), src, own, to_yh)
-        send((tag, "zp", 0, 1), src, own, to["zp"])
-        send((tag, "zm", 0, 1), src, own, to["zm"])
+        for u in range(len(PIECES)):
+            piece = src.at[pl.ds(*PIECES[u])]
+            for d in ("p", "m"):
+                send((tag, d, 0, 1, u), piece, at(Bb, ft, u), to[d])
+        send((tag, "y", 0), src, own, to_yh)
 
     def ev_yl(tag, A):
         i = dpi(1, 0)
@@ -167,12 +179,8 @@
         send((tag, "c", 1, 0), at(A, i), at(A, i), to_core)
         return i
 
-    def ev_yh(tag, Bb):
-        i = fti(1, 0)
-        recv((tag, "yh"), at(Bb, i))
-        send((tag, "zp", 1, 1), at(Bb, i), at(Bb, i), to["zp"])
-        send((tag, "zm", 1, 1), at(Bb, i), at(Bb, i), to["zm"])
-        return i
+    def ev_y0(tag, Bb):
+        recv((tag, "y", 0), at(Bb, fti(1, 0)))
 
     def ev_x(tag, A, d, r, h):
         dx = (-SIGN[d] * h) % NX
@@ -184,10 +192,30 @@
         return i
 
     def ev_z(tag, Bb, d, r, h):
-        i = fti(r, -SIGN[d] * h)
-        recv((tag, d, r, h), at(Bb, i))
-        if h < KZ[d, r]:
-            send((tag, d, r, h + 1), at(Bb, i), at(Bb, i), to[d])
+        sign = 1 if d == "p" else -1
+        i = fti(r, -sign * h)
+        for u in range(len(PIECES)):
+            piece = at(Bb, i, u)
+            recv((tag, d, r, h, u), piece)
+            if h < (4 if d == "p" else 3):
+                send((tag, d, r, h + 1, u), piece, piece, to[d])
+            if r == 0 and (d, h) in (("m", 1), ("p", 2)):
+                send((tag, "y", d, h, u), piece, piece, to_yh)
+        if r == 0 and (d, h) == ("p", 2):
+            early = at(Bb, fti(0, -1))
+            send((tag, "y", "p", 1), early, early, to_yh)
+        return i
+
+    def ev_y(tag, Bb, d, h):
+        sign = 1 if d == "p" else -1
+        i = fti(1, -sign * h)
+        if (d, h) == ("p", 1):
+            recv((tag, "y", d, h), at(Bb, i))
+            return i
+        for u in range(len(PIECES)):
+            piece = at(Bb, i, u)
+            recv((tag, "y", d, h, u), piece)
+            send((tag, d, 1, h + 1, u), piece, piece, to[d])
         return i
 
     def ev_c(tag, A, r, dx):
@@ -242,32 +270,33 @@
     def gc(r, dx):
         moments(V1, M1, ev_c("g", V1, r, dx))
 
-    gz("zp", 0, 1)
-    gz("zm", 0, 1)
+    gz("p", 0, 1)
+    gz("m", 0, 1)
     moments(V1, M1, ev_yl("g", V1))
     gx("xp", 0, 1)
     gx("xm", 0, 1)
-    moments(V2, M2, ev_yh("g", V2))
-    gz("zp", 0, 2)
-    gz("zm", 0, 2)
+    ev_y0("g", V2)
+    moments(V2, M2, fti(1, 0))
+    gz("p", 0, 2)
+    gz("m", 0, 2)
     gx("xp", 1, 1)
     gx("xm", 1, 1)
-    gz("zp", 1, 1)
-    gz("zm", 1, 1)
+    moments(V2, M2, ev_y("g", V2, "m", 1))
     gx("xp", 0, 2)
     gx("xm", 1, 2)
-    gz("zp", 0, 3)
-    gz("zm", 0, 3)
-    gz("zp", 1, 2)
-    gz("zm", 1, 2)
+    gz("p", 0, 3)
+    gz("m", 0, 3)
     for r, dx in CORDER:
         gc(r, dx)
-    gz("zp", 0, 4)
-    gz("zp", 1, 3)
-    gz("zm", 1, 3)
+    gz("m", 1, 2)
+    moments(V2, M2, ev_y("g", V2, "p", 2))
+    moments(V2, M2, ev_y("g", V2, "p", 1))
+    gz("p", 0, 4)
+    gz("p", 1, 3)
+    gz("m", 1, 3)
     drain(lambda n: n[1] in ("c", "xp", "xm", "yl"))
     normalize(V1, M1)
-    gz("zm", 1, 4)
+    gz("p", 1, 4)
     drain()
     normalize(V2, M2)
 
@@ -307,31 +336,33 @@
     for k in range(128, T, 128):
         loss_tile = loss_tile + loss[:, k : k + 128]
 
-    def p2(i):
-        return dot_nn(V1[rows(i), :], G[...])
+    def p2(i, u):
+        return dot_nn(V1[pl.ds(pl.multiple_of(i * R + PIECES[u][0], 16), PIECES[u][1]), :], G[...])
 
     def p1(i):
         return dot_nt(V2[rows(i), :], G[...])
 
-    def zc(d, r, s):
-        i = fti(r, SIGN[d] * (KZ[d, r] - s))
-        val = p2(i)
-        if s:
-            prev = ZSLOT[d, r, s - 1]
-            recv(("s", d, r, s - 1), zr.at[prev])
-            val = val + zr[prev].astype(f32)
-        slot = ZSLOT[d, r, s]
-        zs[slot] = val.astype(bf16)
-        send(("s", d, r, s), zs.at[slot], zr.at[slot], to[d])
-
-    def z_end(r):
-        val = p2(fti(r, 0))
-        for d in ("zp", "zm"):
-            last = KZ[d, r] - 1
-            slot = ZSLOT[d, r, last]
-            recv(("s", d, r, last), zr.at[slot])
-            val = val + zr[slot].astype(f32)
-        return val
+    def arrived(key, u):
+        slot = ZSLOT[key]
+        recv(("s", key, u), part(zr, slot, u))
+        return part(zr, slot, u)[...].astype(f32)
+
+    def zc(r, k, over_y=False, take=()):
+        key = ("y", k) if over_y else (r, k)
+        dev = to_yh if over_y else to["m"] if k > 0 else to["p"]
+        for u in range(len(PIECES)):
+            val = p2(fti(r, -k), u)
+            for source in take:
+                val = val + arrived(source, u)
+            part(zs, ZSLOT[key], u)[...] = val.astype(bf16)
+            send(("s", key, u), part(zs, ZSLOT[key], u), part(zr, ZSLOT[key], u), dev)
+
+    def z_end():
+        for u in range(len(PIECES)):
+            val = p2(fti(0, 0), u)
+            for source in ((0, 1), (0, -1), ("y", 0)):
+                val = val + arrived(source, u)
+            U2[pl.ds(*PIECES[u]), :] = val
 
     def core_send(r, dx):
         slot = CSLOT[r, dx]
@@ -364,10 +395,10 @@
             val = val + xr[slot].astype(f32)
         return val
 
-    zc("zp", 0, 0)
-    zc("zm", 1, 0)
-    zc("zp", 1, 0)
-    zc("zm", 0, 0)
+    zc(1, 4)
+    zc(1, -3)
+    zc(0, 4)
+    zc(0, -3)
     for r, dx in CORDER:
         core_send(r, dx)
 
@@ -402,26 +433,28 @@
     put(0)
     xc("xp", 0, 0)
     xc("xm", 1, 0)
-    zc("zp", 0, 1)
-    zc("zm", 1, 1)
+    zc(1, 1, True)
+    zc(1, 3, take=[(1, 4)])
+    zc(1, -2, take=[(1, -3)])
     take(0)
     put(1)
     xc("xp", 1, 0)
     xc("xm", 0, 0)
-    zc("zp", 1, 1)
-    zc("zm", 0, 1)
+    zc(0, 3, take=[(0, 4)])
+    zc(0, -2, take=[(0, -3)])
     take(1)
     put(2)
+    zc(1, 2, True, take=[(1, 3)])
+    zc(1, -1, True, take=[(1, -2)])
     xc("xp", 0, 1)
     xc("xm", 1, 1)
-    zc("zp", 0, 2)
-    zc("zm", 1, 2)
     take(2)
     put(3)
+    zc(1, 0, True)
     ys[0] = x_end(1).astype(bf16)
     send(("s", "yl"), ys.at[0], yr.at[0], to_yl)
-    zc("zp", 1, 2)
-    zc("zm", 0, 2)
+    zc(0, 2, take=[(0, 3), ("y", 2)])
+    zc(0, -1, take=[(0, -2), ("y", -1)])
     take(3)
 
     def delta(U, V, M, A, D, i):
@@ -444,8 +477,7 @@
     U1[...] = val + yr[0].astype(f32)
     delta(U1, V1, M1, A1, D1, dp)
     start_a("d", D1, at(D1, dp))
-    zc("zp", 0, 3)
-    zc("zm", 1, 3)
+    zc(0, 1, take=[(0, 2), ("y", 1)])
 
     AL[0] = A1[4, :, T : T + 128]
 
@@ -457,16 +489,12 @@
         AL[n + 1] = AL[n] + RL[n]
 
     put_l(0)
-    ys[1] = z_end(1).astype(bf16)
-    send(("s", "yh"), ys.at[1], yr.at[1], to_yh)
     ev_yl("d", D1)
     ev_x("d", D1, "xp", 0, 1)
     ev_x("d", D1, "xm", 0, 1)
     take_l(0)
     put_l(1)
-    val = z_end(0)
-    recv(("s", "yh"), yr.at[1])
-    U2[...] = val + yr[1].astype(f32)
+    z_end()
     delta(U2, V2, M2, A2, D2, ft)
     start_b("d", D2, at(D2, ft))
 
@@ -476,42 +504,53 @@
     ev_x("d", D1, "xm", 1, 2)
     take_l(1)
     put_l(2)
-    ev_z("d", D2, "zp", 0, 1)
-    ev_z("d", D2, "zm", 0, 1)
+    local[2].wait()
+    local[3].wait()
+
+    def weight(w_ref, X, D, i, first=False):
+        term = dot_tn(X[rows(i), :], D[rows(i), :])
+        if first:
+            w_ref[...] = term
+        else:
+            w_ref[...] += term
+
+    def dz(d, r, h):
+        weight(w2_ref, X2, D2, ev_z("d", D2, d, r, h))
+
+    def dy(d, h):
+        weight(w2_ref, X2, D2, ev_y("d", D2, d, h))
+
+    weight(w2_ref, X2, D2, ft, True)
+    dz("p", 0, 1)
+    dz("m", 0, 1)
     take_l(2)
     put_l(3)
-    ev_yh("d", D2)
-    ev_z("d", D2, "zp", 0, 2)
-    ev_z("d", D2, "zm", 0, 2)
+    ev_y0("d", D2)
+    weight(w2_ref, X2, D2, fti(1, 0))
+    for r, dx in CORDER:
+        ev_c("d", D1, r, dx)
+    dz("p", 0, 2)
+    dz("m", 0, 2)
     take_l(3)
     loss_ref[0] = jnp.sum(AL[4]) / F
-    for r, dx in CORDER:
-        ev_c("d", D1, r, dx)
-    local[2].wait()
-    local[3].wait()
-
-    def weights(w_ref, X, D):
-        w_ref[...] = dot_tn(X[0:KC, :], D[0:KC, :])
-
-        def body(k, carry):
-            at_ = pl.ds(pl.multiple_of(k * KC, 16), KC)
-            w_ref[...] += dot_tn(X[at_, :], D[at_, :])
-            return carry
-
-        lax.fori_loop(1, B // KC, body, 0)
-
-    ev_z("d", D2, "zp", 1, 1)
-    ev_z("d", D2, "zm", 1, 1)
-    ev_z("d", D2, "zp", 0, 3)
-    ev_z("d", D2, "zm", 0, 3)
-    weights(w1_ref, X1, D1)
-    ev_z("d", D2, "zp", 1, 2)
-    ev_z("d", D2, "zm", 1, 2)
-    ev_z("d", D2, "zp", 0, 4)
-    ev_z("d", D2, "zp", 1, 3)
-    ev_z("d", D2, "zm", 1, 3)
-    ev_z("d", D2, "zm", 1, 4)
-    weights(w2_ref, X2, D2)
+    dy("m", 1)
+    dz("p", 0, 3)
+    dz("m", 0, 3)
+    w1_ref[...] = dot_tn(X1[0:KC, :], D1[0:KC, :])
+
+    def body(k, carry):
+        at_ = pl.ds(pl.multiple_of(k * KC, 16), KC)
+        w1_ref[...] += dot_tn(X1[at_, :], D1[at_, :])
+        return carry
+
+    lax.fori_loop(1, B // KC, body, 0)
+    dz("m", 1, 2)
+    dy("p", 2)
+    dy("p", 1)
+    dz("p", 0, 4)
+    dz("p", 1, 3)
+    dz("m", 1, 3)
+    dz("p", 1, 4)
     drain()
     assert len(names) <= NSEM
 
@@ -545,8 +584,8 @@
         kernel,
         out_shape=(
             jax.ShapeDtypeStruct((1,), f32),
-            jax.ShapeDtypeStruct((T, T), f32),
-            jax.ShapeDtypeStruct((T, T), f32),
+            V((T, T), f32),
+            V((T, T), f32),
         ),
         in_specs=[anywhere] * 4 + [smem],
         out_specs=(smem, vmem, vmem),

time: 165 us -> 154 us (0.933); the launches traced: 164 us -> 151 us
  Pallas kernels: 156 us -> 146 us
  local copies, waits for them, and re-layouts: 4.52 us -> 1.94 us
    pallas_call x1, Pallas kernels: 156 us -> 146 us  [per_device(): pl.pallas_call(kernel, out_shape=(jax.ShapeDtypeStruct((1,), f32), V((T,...]
    unnamed x2, local copies, waits for them, and re-layouts: 4.52 us -> 1.94 us
where the time goes in v2:
time: 154 us; the launch traced here: 151 us
  Pallas kernels  146 us (95%)
  between operations  2.98 us (2%)
  local copies, waits for them, and re-layouts  1.94 us (1%)
    pallas_call x1, Pallas kernels, per_device(): pl.pallas_call(kernel, out_shape=(jax.ShapeDtypeStruct((1,), f32), V((T,...  146 us

profile of v2, /device:TPU:6, one launch (start us, length us, event | category | flops | bytes accessed | tf_op | source)
XLA Modules:
  0.0 151.0 jit_solution(4038903220044403227)
XLA Ops:
  1.3 146.1 %shard_map.76 = (f32[1]{0:T(128)}, f32[512,512]{1,0:T(8,128)S(1)}, f32[512,512]{1,0:T(8,128)S(1)}) custom-call(bf16[240,512]{1,0:T(8,128)(2,1)} %view1.1, bf16[240,512]{1,0:T(8,128)(2,1)} %view2.1, bf16[3840,512]{1,0:T(8,128)(2,1)} %in1.1, bf16[3840,512]{1,0:T(8,128)(2,1)} %in2.1, f32[1]{0:T(128)S(6)} %copy.13.scale_ref), custom_call_target="tpu_custom_call" | custom-call | flops 10066329600 | bytes 9961472 | tf_op jit(solution)/shard_map/pallas_call | solution.py:583
  147.3 1.0 copy.11
  148.3 1.0 copy.12

commit v3 on v2

--- a/solution.py
+++ b/solution.py
@@ -17,6 +17,7 @@
 SIGN = {"xp": 1, "xm": -1}
 KX = {("xp", 0): 2, ("xm", 0): 1, ("xp", 1): 1, ("xm", 1): 2}
 PIECES = ((0, 128), (128, 112))
+NP = len(PIECES)
 ZSLOT = {
     key: n
     for n, key in enumerate(
@@ -30,7 +31,40 @@
         XSLOT[key + (hop,)] = len(XSLOT)
 CORDER = [(0, 2), (1, 2), (1, 1), (0, 3), (0, 1), (1, 3), (1, 0), (0, 0)]
 CSLOT = {key: n for n, key in enumerate(CORDER)}
-NSEM = 200
+NSEM = 240
+
+def both_z(r, hp, hm):
+    return [("z", d, r, h, u) for u in range(NP) for d, h in (("p", hp), ("m", hm)) if h]
+
+
+def one_z(d, r, h):
+    return [("z", d, r, h, u) for u in range(NP)]
+
+
+def over_y(d, h):
+    return [("y", d, h, u) for u in range(NP)]
+
+
+ORDER = (
+    both_z(0, 1, 1)
+    + [("yl",), ("x", "xp", 0, 1), ("x", "xm", 0, 1)]
+    + both_z(0, 2, 2)
+    + [("x", "xp", 1, 1), ("x", "xm", 1, 1)]
+    + over_y("m", 1)
+    + [("ls", 0)]
+    + both_z(0, 3, 3)
+    + [("x", "xp", 0, 2), ("x", "xm", 1, 2)]
+    + over_y("p", 2)
+    + [("ls", 1)]
+    + one_z("m", 1, 2)
+    + [("c", r, dx) for r, dx in CORDER]
+    + one_z("p", 0, 4)
+    + one_z("p", 1, 3)
+    + one_z("m", 1, 3)
+    + [("lr", 0), ("lr", 1)]
+    + one_z("p", 1, 4)
+)
+NORM = len(ORDER) - 2 - 4 * NP
 
 
 def dot_tn(left, right):
@@ -164,12 +198,9 @@
         send((tag, "c", 0, 0), src, own, to_core)
 
     def start_b(tag, Bb, src):
-        own = at(Bb, ft)
         for u in range(len(PIECES)):
-            piece = src.at[pl.ds(*PIECES[u])]
             for d in ("p", "m"):
-                send((tag, d, 0, 1, u), piece, at(Bb, ft, u), to[d])
-        send((tag, "y", 0), src, own, to_yh)
+                send((tag, d, 0, 1, u), src.at[pl.ds(*PIECES[u])], at(Bb, ft, u), to[d])
 
     def ev_yl(tag, A):
         i = dpi(1, 0)
@@ -179,8 +210,22 @@
         send((tag, "c", 1, 0), at(A, i), at(A, i), to_core)
         return i
 
-    def ev_y0(tag, Bb):
-        recv((tag, "y", 0), at(Bb, fti(1, 0)))
+    def ev_z(tag, Bb, d, r, h, u):
+        i = fti(r, -h if d == "p" else h)
+        piece = at(Bb, i, u)
+        recv((tag, d, r, h, u), piece)
+        if r == 0 and (d, h) in (("m", 1), ("p", 2)):
+            send((tag, "y", d, h, u), piece, piece, to_yh)
+        if h < (4 if d == "p" else 3):
+            send((tag, d, r, h + 1, u), piece, piece, to[d])
+        return i
+
+    def ev_y(tag, Bb, d, h, u):
+        i = fti(1, -h if d == "p" else h)
+        piece = at(Bb, i, u)
+        recv((tag, "y", d, h, u), piece)
+        send((tag, d, 1, h + 1, u), piece, piece, to[d])
+        return i
 
     def ev_x(tag, A, d, r, h):
         dx = (-SIGN[d] * h) % NX
@@ -191,32 +236,39 @@
         send((tag, "c", r, dx), at(A, i), at(A, i), to_core)
         return i
 
-    def ev_z(tag, Bb, d, r, h):
-        sign = 1 if d == "p" else -1
-        i = fti(r, -sign * h)
-        for u in range(len(PIECES)):
-            piece = at(Bb, i, u)
-            recv((tag, d, r, h, u), piece)
-            if h < (4 if d == "p" else 3):
-                send((tag, d, r, h + 1, u), piece, piece, to[d])
-            if r == 0 and (d, h) in (("m", 1), ("p", 2)):
-                send((tag, "y", d, h, u), piece, piece, to_yh)
-        if r == 0 and (d, h) == ("p", 2):
-            early = at(Bb, fti(0, -1))
-            send((tag, "y", "p", 1), early, early, to_yh)
+    def late_send(tag, Bb, n):
+        block = at(Bb, fti(0, -n))
+        send((tag, "y", n), block, block, to_yh)
+
+    def late_recv(tag, Bb, n):
+        i = fti(1, -n)
+        recv((tag, "y", n), at(Bb, i))
         return i
 
-    def ev_y(tag, Bb, d, h):
-        sign = 1 if d == "p" else -1
-        i = fti(1, -sign * h)
-        if (d, h) == ("p", 1):
-            recv((tag, "y", d, h), at(Bb, i))
-            return i
-        for u in range(len(PIECES)):
-            piece = at(Bb, i, u)
-            recv((tag, "y", d, h, u), piece)
-            send((tag, d, 1, h + 1, u), piece, piece, to[d])
-        return i
+    def gather(order, tag, A, Bb, hook_a, hook_b):
+        last = len(PIECES) - 1
+        for ev in order:
+            kind, args = ev[0], ev[1:]
+            if kind == "z":
+                i = ev_z(tag, Bb, *args)
+                if args[-1] == last:
+                    hook_b(i)
+            elif kind == "y":
+                i = ev_y(tag, Bb, *args)
+                if args[-1] == last:
+                    hook_b(i)
+            elif kind == "ls":
+                late_send(tag, Bb, *args)
+            elif kind == "lr":
+                hook_b(late_recv(tag, Bb, *args))
+            elif kind == "yl":
+                hook_a(ev_yl(tag, A))
+            elif kind == "x":
+                hook_a(ev_x(tag, A, *args))
+            elif kind == "c":
+                hook_a(ev_c(tag, A, *args))
+            else:
+                kind()
 
     def ev_c(tag, A, r, dx):
         i = dpi(r, dx, 1)
@@ -261,42 +313,12 @@
     moments(V1, M1, dp)
     moments(V2, M2, ft)
 
-    def gz(d, r, h):
-        moments(V2, M2, ev_z("g", V2, d, r, h))
-
-    def gx(d, r, h):
-        moments(V1, M1, ev_x("g", V1, d, r, h))
-
-    def gc(r, dx):
-        moments(V1, M1, ev_c("g", V1, r, dx))
-
-    gz("p", 0, 1)
-    gz("m", 0, 1)
-    moments(V1, M1, ev_yl("g", V1))
-    gx("xp", 0, 1)
-    gx("xm", 0, 1)
-    ev_y0("g", V2)
-    moments(V2, M2, fti(1, 0))
-    gz("p", 0, 2)
-    gz("m", 0, 2)
-    gx("xp", 1, 1)
-    gx("xm", 1, 1)
-    moments(V2, M2, ev_y("g", V2, "m", 1))
-    gx("xp", 0, 2)
-    gx("xm", 1, 2)
-    gz("p", 0, 3)
-    gz("m", 0, 3)
-    for r, dx in CORDER:
-        gc(r, dx)
-    gz("m", 1, 2)
-    moments(V2, M2, ev_y("g", V2, "p", 2))
-    moments(V2, M2, ev_y("g", V2, "p", 1))
-    gz("p", 0, 4)
-    gz("p", 1, 3)
-    gz("m", 1, 3)
-    drain(lambda n: n[1] in ("c", "xp", "xm", "yl"))
-    normalize(V1, M1)
-    gz("p", 1, 4)
+    def early_normalize():
+        drain(lambda n: n[1] in ("c", "xp", "xm", "yl"))
+        normalize(V1, M1)
+
+    order = ORDER[:NORM] + [(early_normalize,)] + ORDER[NORM:]
+    gather(order, "g", V1, V2, lambda i: moments(V1, M1, i), lambda i: moments(V2, M2, i))
     drain()
     normalize(V2, M2)
 
@@ -397,10 +419,12 @@
 
     zc(1, 4)
     zc(1, -3)
+    zc(1, 1, True)
+    zc(1, 0, True)
+    for r, dx in CORDER:
+        core_send(r, dx)
     zc(0, 4)
     zc(0, -3)
-    for r, dx in CORDER:
-        core_send(r, dx)
 
     ones = jnp.ones((16, T), bf16)
     second1 = dot_nt(ones, GH[...]) + dot_nt(ones, GL[...])
@@ -433,7 +457,6 @@
     put(0)
     xc("xp", 0, 0)
     xc("xm", 1, 0)
-    zc(1, 1, True)
     zc(1, 3, take=[(1, 4)])
     zc(1, -2, take=[(1, -3)])
     take(0)
@@ -442,20 +465,19 @@
     xc("xm", 0, 0)
     zc(0, 3, take=[(0, 4)])
     zc(0, -2, take=[(0, -3)])
+    zc(1, 2, True, take=[(1, 3)])
+    zc(1, -1, True, take=[(1, -2)])
     take(1)
     put(2)
-    zc(1, 2, True, take=[(1, 3)])
-    zc(1, -1, True, take=[(1, -2)])
     xc("xp", 0, 1)
     xc("xm", 1, 1)
     take(2)
     put(3)
-    zc(1, 0, True)
     ys[0] = x_end(1).astype(bf16)
     send(("s", "yl"), ys.at[0], yr.at[0], to_yl)
+    take(3)
     zc(0, 2, take=[(0, 3), ("y", 2)])
     zc(0, -1, take=[(0, -2), ("y", -1)])
-    take(3)
 
     def delta(U, V, M, A, D, i):
         stats = A[4]
@@ -489,21 +511,12 @@
         AL[n + 1] = AL[n] + RL[n]
 
     put_l(0)
-    ev_yl("d", D1)
-    ev_x("d", D1, "xp", 0, 1)
-    ev_x("d", D1, "xm", 0, 1)
     take_l(0)
     put_l(1)
     z_end()
     delta(U2, V2, M2, A2, D2, ft)
     start_b("d", D2, at(D2, ft))
 
-    ev_x("d", D1, "xp", 1, 1)
-    ev_x("d", D1, "xm", 1, 1)
-    ev_x("d", D1, "xp", 0, 2)
-    ev_x("d", D1, "xm", 1, 2)
-    take_l(1)
-    put_l(2)
     local[2].wait()
     local[3].wait()
 
@@ -514,43 +527,33 @@
         else:
             w_ref[...] += term
 
-    def dz(d, r, h):
-        weight(w2_ref, X2, D2, ev_z("d", D2, d, r, h))
-
-    def dy(d, h):
-        weight(w2_ref, X2, D2, ev_y("d", D2, d, h))
+    def weights_one():
+        w1_ref[...] = dot_tn(X1[0:KC, :], D1[0:KC, :])
+
+        def body(k, carry):
+            at_ = pl.ds(pl.multiple_of(k * KC, 16), KC)
+            w1_ref[...] += dot_tn(X1[at_, :], D1[at_, :])
+            return carry
+
+        lax.fori_loop(1, B // KC, body, 0)
+
+    def loss_step(n):
+        def step():
+            take_l(n)
+            if n < 3:
+                put_l(n + 1)
+            else:
+                loss_ref[0] = jnp.sum(AL[4]) / F
+
+        return (step,)
 
     weight(w2_ref, X2, D2, ft, True)
-    dz("p", 0, 1)
-    dz("m", 0, 1)
-    take_l(2)
-    put_l(3)
-    ev_y0("d", D2)
-    weight(w2_ref, X2, D2, fti(1, 0))
-    for r, dx in CORDER:
-        ev_c("d", D1, r, dx)
-    dz("p", 0, 2)
-    dz("m", 0, 2)
-    take_l(3)
-    loss_ref[0] = jnp.sum(AL[4]) / F
-    dy("m", 1)
-    dz("p", 0, 3)
-    dz("m", 0, 3)
-    w1_ref[...] = dot_tn(X1[0:KC, :], D1[0:KC, :])
-
-    def body(k, carry):
-        at_ = pl.ds(pl.multiple_of(k * KC, 16), KC)
-        w1_ref[...] += dot_tn(X1[at_, :], D1[at_, :])
-        return carry
-
-    lax.fori_loop(1, B // KC, body, 0)
-    dz("m", 1, 2)
-    dy("p", 2)
-    dy("p", 1)
-    dz("p", 0, 4)
-    dz("p", 1, 3)
-    dz("m", 1, 3)
-    dz("p", 1, 4)
+    order = (
+        ORDER[: 2 * NP] + [loss_step(1)] + ORDER[2 * NP : 4 * NP + 3] + [loss_step(2)]
+        + ORDER[4 * NP + 3 : NORM] + [(weights_one,)] + ORDER[NORM : NORM + NP]
+        + [loss_step(3)] + ORDER[NORM + NP :]
+    )
+    gather(order, "d", D1, D2, lambda i: None, lambda i: weight(w2_ref, X2, D2, i))
     drain()
     assert len(names) <= NSEM
 
@@ -569,7 +572,7 @@
         V((len(ZSLOT),) + block, bf16), V((len(ZSLOT),) + block, bf16),
         V((len(CSLOT),) + block, bf16), V((len(CSLOT),) + block, bf16),
         V((len(XSLOT),) + block, bf16), V((len(XSLOT),) + block, bf16),
-        V((2,) + block, bf16), V((2,) + block, bf16),
+        V((1,) + block, bf16), V((1,) + block, bf16),
         V(block, f32), V(block, f32),
         V((T, T), f32), V((T, T), bf16), V((T, T), bf16), V((T, T), bf16),
         V((32, T), f32), V((32, T), f32),

time: 154 us -> 132 us (0.86); the launches traced: 151 us -> 132 us
  Pallas kernels: 146 us -> 127 us
    pallas_call x1, Pallas kernels: 146 us -> 127 us  [per_device(): pl.pallas_call(kernel, out_shape=(jax.ShapeDtypeStruct((1,), f32), V((T,...]
where the time goes in v3:
time: 132 us
  Pallas kernels  127 us (96%)
  between operations  2.98 us (2%)
  local copies, waits for them, and re-layouts  1.94 us (1%)
    pallas_call x1, Pallas kernels, per_device(): pl.pallas_call(kernel, out_shape=(jax.ShapeDtypeStruct((1,), f32), V((T,...  127 us

profile of v3, /device:TPU:6, one launch (start us, length us, event | category | flops | bytes accessed | tf_op | source)
XLA Modules:
  0.0 131.7 jit_solution(10860010751531283672)
XLA Ops:
  1.3 126.8 %shard_map.76 = (f32[1]{0:T(128)}, f32[512,512]{1,0:T(8,128)S(1)}, f32[512,512]{1,0:T(8,128)S(1)}) custom-call(bf16[240,512]{1,0:T(8,128)(2,1)} %view1.1, bf16[240,512]{1,0:T(8,128)(2,1)} %view2.1, bf16[3840,512]{1,0:T(8,128)(2,1)} %in1.1, bf16[3840,512]{1,0:T(8,128)(2,1)} %in2.1, f32[1]{0:T(128)S(6)} %copy.13.scale_ref), custom_call_target="tpu_custom_call" | custom-call | flops 10066329600 | bytes 9961472 | tf_op jit(solution)/shard_map/pallas_call | solution.py:586
  128.1 1.0 copy.11
  129.1 1.0 copy.12

commit v4 on v3

--- a/solution.py
+++ b/solution.py
@@ -45,26 +45,22 @@
     return [("y", d, h, u) for u in range(NP)]
 
 
-ORDER = (
-    both_z(0, 1, 1)
-    + [("yl",), ("x", "xp", 0, 1), ("x", "xm", 0, 1)]
-    + both_z(0, 2, 2)
-    + [("x", "xp", 1, 1), ("x", "xm", 1, 1)]
-    + over_y("m", 1)
-    + [("ls", 0)]
-    + both_z(0, 3, 3)
-    + [("x", "xp", 0, 2), ("x", "xm", 1, 2)]
-    + over_y("p", 2)
-    + [("ls", 1)]
-    + one_z("m", 1, 2)
-    + [("c", r, dx) for r, dx in CORDER]
-    + one_z("p", 0, 4)
-    + one_z("p", 1, 3)
-    + one_z("m", 1, 3)
-    + [("lr", 0), ("lr", 1)]
-    + one_z("p", 1, 4)
-)
-NORM = len(ORDER) - 2 - 4 * NP
+ORDER = [
+    both_z(0, 1, 1),
+    [("yl",), ("x", "xp", 0, 1), ("x", "xm", 0, 1)],
+    both_z(0, 2, 2),
+    [("x", "xp", 1, 1), ("x", "xm", 1, 1)] + over_y("m", 1) + [("ls", 0)],
+    both_z(0, 3, 3),
+    [("x", "xp", 0, 2), ("x", "xm", 1, 2)] + over_y("p", 2) + [("ls", 1)],
+    one_z("m", 1, 2),
+    [("c", r, dx) for r, dx in CORDER],
+    one_z("p", 0, 4),
+    one_z("p", 1, 3),
+    one_z("m", 1, 3),
+    [("lr", 0), ("lr", 1)],
+    one_z("p", 1, 4),
+]
+WHOLE = 7
 
 
 def dot_tn(left, right):
@@ -89,7 +85,7 @@
 def kernel(
     view1, view2, in1, in2, scale_ref,
     loss_ref, w1_ref, w2_ref,
-    V1, V2, D1, D2, X1, X2,
+    V1, V2, D1, D2, X1, X2, P1, P2, PT,
     zs, zr, cs, cr, xs, xr, ys, yr, U1, U2,
     C, G, GH, GL, M1, M2, A1, R1, A2, R2, AL, RL,
     ssem, rsem, lsem,
@@ -197,10 +193,9 @@
         send((tag, "xm", 0, 1), src, own, to["xm"])
         send((tag, "c", 0, 0), src, own, to_core)
 
-    def start_b(tag, Bb, src):
-        for u in range(len(PIECES)):
-            for d in ("p", "m"):
-                send((tag, d, 0, 1, u), src.at[pl.ds(*PIECES[u])], at(Bb, ft, u), to[d])
+    def start_b(tag, Bb, src, u):
+        for d in ("p", "m"):
+            send((tag, d, 0, 1, u), src.at[pl.ds(*PIECES[u])], at(Bb, ft, u), to[d])
 
     def ev_yl(tag, A):
         i = dpi(1, 0)
@@ -245,30 +240,29 @@
         recv((tag, "y", n), at(Bb, i))
         return i
 
-    def gather(order, tag, A, Bb, hook_a, hook_b):
+    def gather(tag, A, Bb, hook_a, hook_b, after):
         last = len(PIECES) - 1
-        for ev in order:
-            kind, args = ev[0], ev[1:]
-            if kind == "z":
-                i = ev_z(tag, Bb, *args)
-                if args[-1] == last:
-                    hook_b(i)
-            elif kind == "y":
-                i = ev_y(tag, Bb, *args)
-                if args[-1] == last:
-                    hook_b(i)
-            elif kind == "ls":
-                late_send(tag, Bb, *args)
-            elif kind == "lr":
-                hook_b(late_recv(tag, Bb, *args))
-            elif kind == "yl":
-                hook_a(ev_yl(tag, A))
-            elif kind == "x":
-                hook_a(ev_x(tag, A, *args))
-            elif kind == "c":
-                hook_a(ev_c(tag, A, *args))
-            else:
-                kind()
+        for n, group in enumerate(ORDER):
+            work = []
+            for kind, *args in group:
+                if kind == "z" or kind == "y":
+                    i = (ev_z if kind == "z" else ev_y)(tag, Bb, *args)
+                    if args[-1] == last:
+                        work.append((hook_b, i))
+                elif kind == "ls":
+                    late_send(tag, Bb, *args)
+                elif kind == "lr":
+                    work.append((hook_b, late_recv(tag, Bb, *args)))
+                elif kind == "yl":
+                    work.append((hook_a, ev_yl(tag, A)))
+                elif kind == "x":
+                    work.append((hook_a, ev_x(tag, A, *args)))
+                else:
+                    work.append((hook_a, ev_c(tag, A, *args)))
+            for hook, i in work:
+                hook(i)
+            if n in after:
+                after[n]()
 
     def ev_c(tag, A, r, dx):
         i = dpi(r, dx, 1)
@@ -289,11 +283,15 @@
         M[0:8, :] = s
         M[8:16, :] = q
 
-    def normalize(V, M):
+    def statistics(M):
         average = jnp.sum(M[0:8, :], axis=0, keepdims=True) / B
         spread = jnp.sum(M[8:16, :], axis=0, keepdims=True) / B - average * average
-        inv = lax.rsqrt(spread + epsilon)
-        M[16:24, :] = jnp.broadcast_to(inv, (8, T))
+        M[16:24, :] = jnp.broadcast_to(lax.rsqrt(spread + epsilon), (8, T))
+        M[32:40, :] = jnp.broadcast_to(average, (8, T))
+
+    def normalize(V, M):
+        average = M[32:33, :]
+        inv = M[16:17, :]
 
         def body(k, total):
             at_ = pl.ds(pl.multiple_of(k * CH, 16), CH)
@@ -306,40 +304,65 @@
 
     M1[...] = jnp.zeros_like(M1)
     M2[...] = jnp.zeros_like(M2)
-    start_b("g", V2, view2)
+    for u in range(NP):
+        start_b("g", V2, view2, u)
     start_a("g", V1, view1)
     local[0].wait()
     local[1].wait()
     moments(V1, M1, dp)
     moments(V2, M2, ft)
 
-    def early_normalize():
+    ready = []
+    waiting = [ft]
+
+    def corr(i):
+        C[...] += dot_tn(V1[rows(i), :], V2[rows(i), :])
+
+    def work_two(i):
+        moments(V2, M2, i)
+        if ready:
+            corr(i)
+        else:
+            waiting.append(i)
+
+    def some(count):
+        for _ in range(min(count, len(waiting))):
+            corr(waiting.pop(0))
+
+    def first_whole():
         drain(lambda n: n[1] in ("c", "xp", "xm", "yl"))
+        statistics(M1)
         normalize(V1, M1)
-
-    order = ORDER[:NORM] + [(early_normalize,)] + ORDER[NORM:]
-    gather(order, "g", V1, V2, lambda i: moments(V1, M1, i), lambda i: moments(V2, M2, i))
-    drain()
-    normalize(V2, M2)
+        C[...] = jnp.zeros_like(C)
+        ready.append(True)
+        some(4)
+
+    after = {WHOLE: first_whole, WHOLE + 1: lambda: some(2), WHOLE + 2: lambda: some(4), WHOLE + 3: lambda: some(20)}
+    gather("g", V1, V2, lambda i: moments(V1, M1, i), work_two, after)
+    statistics(M2)
 
     KC = 768
-    C[...] = dot_tn(V1[0:KC, :], V2[0:KC, :])
-
-    def corr(k, carry):
-        at_ = pl.ds(pl.multiple_of(k * KC, 16), KC)
-        C[...] += dot_tn(V1[at_, :], V2[at_, :])
-        return carry
-
-    lax.fori_loop(1, B // KC, corr, 0)
+    lane_row = lax.broadcasted_iota(jnp.int32, (16, T), 0)
+
+    def split(value):
+        high = value.astype(bf16).astype(f32)
+        return high, value - high
+
+    s_high, s_low = split(jnp.concatenate([M1[24:32, :], M1[24:32, :]], axis=0))
+    a_high, a_low = split(jnp.concatenate([M2[32:40, :], M2[32:40, :]], axis=0))
+    left = jnp.where(lane_row < 2, s_high, jnp.where(lane_row < 4, s_low, 0.0)).astype(bf16)
+    right = jnp.where(lane_row % 2 == 0, a_high, a_low).astype(bf16)
+    C[...] -= dot_tn(left, right)
 
     CG = 32
     scale = scale_ref[0]
+    inv_two = M2[16:17, :] / B
     row0 = ft * T
     col0 = dp * T
 
     def grad(k, loss):
         at_ = pl.ds(pl.multiple_of(k * CG, CG), CG)
-        corr_ = C[at_, :] / B
+        corr_ = C[at_, :] * inv_two
         row_ids = row0 + k * CG + lax.broadcasted_iota(jnp.int32, (CG, T), 0)
         col_ids = col0 + lax.broadcasted_iota(jnp.int32, (CG, T), 1)
         on = row_ids == col_ids
@@ -358,43 +381,102 @@
     for k in range(128, T, 128):
         loss_tile = loss_tile + loss[:, k : k + 128]
 
+    DC = 16
+
+    def delta(U, V, M, A, D, i, start, count):
+        stats = A[4]
+        first = stats[0:1, 0:T] / B
+        second = stats[1:2, 0:T] / B
+        inv = M[16:17, :]
+
+        def body(k, carry):
+            off = pl.multiple_of(start + k * DC, 16)
+            at_ = pl.ds(pl.multiple_of(i * R + start + k * DC, 16), DC)
+            own = V[at_, :].astype(f32)
+            D[at_, :] = (inv * (U[pl.ds(off, DC), :] / B - first - own * second)).astype(bf16)
+            return carry
+
+        lax.fori_loop(0, count // DC, body, 0)
+
+    def pair2(dz):
+        at_ = pl.ds(pl.multiple_of(fti(0, dz) // 2 * (2 * R), 16), 2 * R)
+        P2[at_, :] = dot_nn(V1[at_, :], G[...])
+
+    def pair1(r, dx):
+        PT[...] = dot_nt(V2[pl.ds(pl.multiple_of(dpi(r, dx) // 2 * (2 * R), 16), 2 * R), :], G[...])
+        P1[CSLOT[r, dx]] = PT[rows(c), :]
+
     def p2(i, u):
-        return dot_nn(V1[pl.ds(pl.multiple_of(i * R + PIECES[u][0], 16), PIECES[u][1]), :], G[...])
-
-    def p1(i):
-        return dot_nt(V2[rows(i), :], G[...])
+        return P2[pl.ds(pl.multiple_of(i * R + PIECES[u][0], 16), PIECES[u][1]), :]
 
     def arrived(key, u):
         slot = ZSLOT[key]
         recv(("s", key, u), part(zr, slot, u))
         return part(zr, slot, u)[...].astype(f32)
 
-    def zc(r, k, over_y=False, take=()):
+    def zc(u, r, k, over_y=False, take=()):
         key = ("y", k) if over_y else (r, k)
         dev = to_yh if over_y else to["m"] if k > 0 else to["p"]
-        for u in range(len(PIECES)):
-            val = p2(fti(r, -k), u)
-            for source in take:
-                val = val + arrived(source, u)
-            part(zs, ZSLOT[key], u)[...] = val.astype(bf16)
-            send(("s", key, u), part(zs, ZSLOT[key], u), part(zr, ZSLOT[key], u), dev)
-
-    def z_end():
-        for u in range(len(PIECES)):
-            val = p2(fti(0, 0), u)
-            for source in ((0, 1), (0, -1), ("y", 0)):
-                val = val + arrived(source, u)
-            U2[pl.ds(*PIECES[u]), :] = val
+        val = p2(fti(r, -k), u)
+        for source in take:
+            val = val + arrived(source, u)
+        part(zs, ZSLOT[key], u)[...] = val.astype(bf16)
+        send(("s", key, u), part(zs, ZSLOT[key], u), part(zr, ZSLOT[key], u), dev)
+
+    def z_end(u):
+        val = p2(fti(0, 0), u)
+        for source in ((0, 1), (0, -1), ("y", 0)):
+            val = val + arrived(source, u)
+        U2[pl.ds(*PIECES[u]), :] = val
+        delta(U2, V2, M2, A2, D2, ft, *PIECES[u])
+        start_b("d", D2, at(D2, ft), u)
+
+    def far(u):
+        if u == 0:
+            pair2(-4)
+            pair2(3)
+        zc(u, 1, 4)
+        zc(u, 1, -3)
+
+    def far_own(u):
+        zc(u, 0, 4)
+        zc(u, 0, -3)
+
+    def middle(u):
+        if u == 0:
+            pair2(-3)
+            pair2(2)
+        zc(u, 1, 3, take=[(1, 4)])
+        zc(u, 1, -2, take=[(1, -3)])
+
+    def middle_own(u):
+        zc(u, 0, 3, take=[(0, 4)])
+        zc(u, 0, -2, take=[(0, -3)])
+
+    def cross(u):
+        if u == 0:
+            pair2(-2)
+            pair2(1)
+        zc(u, 1, 2, True, take=[(1, 3)])
+        zc(u, 1, -1, True, take=[(1, -2)])
+
+    def near(u):
+        zc(u, 0, 2, take=[(0, 3), ("y", 2)])
+        zc(u, 0, -1, take=[(0, -2), ("y", -1)])
+
+    def nearest(u):
+        zc(u, 0, 1, take=[(0, 2), ("y", 1)])
 
     def core_send(r, dx):
+        pair1(r, dx)
         slot = CSLOT[r, dx]
-        cs[slot] = p1(dpi(r, dx, 1)).astype(bf16)
+        cs[slot] = PT[rows(1 - c), :].astype(bf16)
         send(("s", "c", r, dx), cs.at[slot], cr.at[slot], to_core)
 
     def both(r, dx):
         dx = dx % NX
-        val = p1(dpi(r, dx))
         slot = CSLOT[r, dx]
+        val = P1[slot]
         recv(("s", "c", r, dx), cr.at[slot])
         return val + cr[slot].astype(f32)
 
@@ -417,19 +499,27 @@
             val = val + xr[slot].astype(f32)
         return val
 
-    zc(1, 4)
-    zc(1, -3)
-    zc(1, 1, True)
-    zc(1, 0, True)
-    for r, dx in CORDER:
+    far(0)
+    far(1)
+    drain(lambda n: n[0] == "g")
+    normalize(V2, M2)
+    pair2(-1)
+    zc(0, 1, 1, True)
+    zc(1, 1, 1, True)
+    for r, dx in CORDER[0:4]:
         core_send(r, dx)
-    zc(0, 4)
-    zc(0, -3)
+    middle(0)
+    far_own(0)
+    xc("xp", 0, 0)
+    xc("xm", 1, 0)
+    middle(1)
+    for r, dx in CORDER[4:8]:
+        core_send(r, dx)
+    far_own(1)
 
     ones = jnp.ones((16, T), bf16)
     second1 = dot_nt(ones, GH[...]) + dot_nt(ones, GL[...])
     second2 = dot_nn(ones, GH[...]) + dot_nn(ones, GL[...])
-    lane_row = lax.broadcasted_iota(jnp.int32, (16, T), 0)
 
     def split_rows(M):
         s = jnp.concatenate([M[24:32, :], M[24:32, :]], axis=0)
@@ -455,52 +545,34 @@
         A2[n + 1] = A2[n] + R2[n]
 
     put(0)
-    xc("xp", 0, 0)
-    xc("xm", 1, 0)
-    zc(1, 3, take=[(1, 4)])
-    zc(1, -2, take=[(1, -3)])
+    cross(0)
+    xc("xp", 1, 0)
+    xc("xm", 0, 0)
+    middle_own(0)
     take(0)
     put(1)
-    xc("xp", 1, 0)
-    xc("xm", 0, 0)
-    zc(0, 3, take=[(0, 4)])
-    zc(0, -2, take=[(0, -3)])
-    zc(1, 2, True, take=[(1, 3)])
-    zc(1, -1, True, take=[(1, -2)])
+    cross(1)
+    middle_own(1)
+    xc("xp", 0, 1)
+    xc("xm", 1, 1)
     take(1)
     put(2)
-    xc("xp", 0, 1)
-    xc("xm", 1, 1)
+    pair2(0)
+    zc(0, 1, 0, True)
+    zc(1, 1, 0, True)
+    near(0)
     take(2)
     put(3)
     ys[0] = x_end(1).astype(bf16)
     send(("s", "yl"), ys.at[0], yr.at[0], to_yl)
+    near(1)
     take(3)
-    zc(0, 2, take=[(0, 3), ("y", 2)])
-    zc(0, -1, take=[(0, -2), ("y", -1)])
-
-    def delta(U, V, M, A, D, i):
-        stats = A[4]
-        first = stats[0:1, 0:T] / B
-        second = stats[1:2, 0:T] / B
-        inv = M[16:17, :]
-
-        def body(k, carry):
-            off = pl.multiple_of(k * CH, 16)
-            at_ = pl.ds(pl.multiple_of(i * R + k * CH, 16), CH)
-            own = V[at_, :].astype(f32)
-            D[at_, :] = (inv * (U[pl.ds(off, CH), :] / B - first - own * second)).astype(bf16)
-            return carry
-
-        lax.fori_loop(0, R // CH, body, 0)
-
+    nearest(0)
     val = x_end(0)
     recv(("s", "yl"), yr.at[0])
     U1[...] = val + yr[0].astype(f32)
-    delta(U1, V1, M1, A1, D1, dp)
+    delta(U1, V1, M1, A1, D1, dp, 0, R)
     start_a("d", D1, at(D1, dp))
-    zc(0, 1, take=[(0, 2), ("y", 1)])
-
     AL[0] = A1[4, :, T : T + 128]
 
     def put_l(n):
@@ -511,12 +583,11 @@
         AL[n + 1] = AL[n] + RL[n]
 
     put_l(0)
+    nearest(1)
+    z_end(0)
     take_l(0)
     put_l(1)
-    z_end()
-    delta(U2, V2, M2, A2, D2, ft)
-    start_b("d", D2, at(D2, ft))
-
+    z_end(1)
     local[2].wait()
     local[3].wait()
 
@@ -538,22 +609,15 @@
         lax.fori_loop(1, B // KC, body, 0)
 
     def loss_step(n):
-        def step():
-            take_l(n)
-            if n < 3:
-                put_l(n + 1)
-            else:
-                loss_ref[0] = jnp.sum(AL[4]) / F
-
-        return (step,)
+        take_l(n)
+        if n < 3:
+            put_l(n + 1)
+        else:
+            loss_ref[0] = jnp.sum(AL[4]) / F
 
     weight(w2_ref, X2, D2, ft, True)
-    order = (
-        ORDER[: 2 * NP] + [loss_step(1)] + ORDER[2 * NP : 4 * NP + 3] + [loss_step(2)]
-        + ORDER[4 * NP + 3 : NORM] + [(weights_one,)] + ORDER[NORM : NORM + NP]
-        + [loss_step(3)] + ORDER[NORM + NP :]
-    )
-    gather(order, "d", D1, D2, lambda i: None, lambda i: weight(w2_ref, X2, D2, i))
+    after = {0: lambda: loss_step(1), 2: lambda: loss_step(2), 4: lambda: loss_step(3), WHOLE: weights_one}
+    gather("d", D1, D2, lambda i: None, lambda i: weight(w2_ref, X2, D2, i), after)
     drain()
     assert len(names) <= NSEM
 
@@ -568,14 +632,14 @@
     V = pltpu.VMEM
     scratch = [
         V((B, T), bf16), V((B, T), bf16), V((B, T), bf16), V((B, T), bf16),
-        V((B, T), bf16), V((B, T), bf16),
+        V((B, T), bf16), V((B, T), bf16), V((len(CSLOT),) + block, f32), V((B, T), f32), V((2 * R, T), f32),
         V((len(ZSLOT),) + block, bf16), V((len(ZSLOT),) + block, bf16),
         V((len(CSLOT),) + block, bf16), V((len(CSLOT),) + block, bf16),
         V((len(XSLOT),) + block, bf16), V((len(XSLOT),) + block, bf16),
         V((1,) + block, bf16), V((1,) + block, bf16),
         V(block, f32), V(block, f32),
         V((T, T), f32), V((T, T), bf16), V((T, T), bf16), V((T, T), bf16),
-        V((32, T), f32), V((32, T), f32),
+        V((40, T), f32), V((40, T), f32),
         V((5, 8, T + 128), f32), V((4, 8, T + 128), f32),
         V((5, 8, T), f32), V((4, 8, T), f32),
         V((5, 8, 128), f32), V((4, 8, 128), f32),
@@ -594,7 +658,7 @@
         out_specs=(smem, vmem, vmem),
         scratch_shapes=scratch,
         compiler_params=pltpu.CompilerParams(
-            collective_id=0, has_side_effects=True, vmem_limit_bytes=58 * 1024 * 1024
+            collective_id=0, has_side_effects=True, vmem_limit_bytes=59 * 1024 * 1024
         ),
         cost_estimate=pl.CostEstimate(
             flops=10 * B * T * T, bytes_accessed=4 * B * T + 8 * T * T, transcendentals=0

time: 132 us -> 128 us (0.970)
  Pallas kernels: 127 us -> 122 us
    pallas_call x1, Pallas kernels: 127 us -> 122 us  [per_device(): pl.pallas_call(kernel, out_shape=(jax.ShapeDtypeStruct((1,), f32), V((T,...]
where the time goes in v4:
time: 128 us; the launch traced here: 127 us
  Pallas kernels  122 us (95%)
  between operations  2.98 us (2%)
  local copies, waits for them, and re-layouts  1.94 us (2%)
    pallas_call x1, Pallas kernels, per_device(): pl.pallas_call(kernel, out_shape=(jax.ShapeDtypeStruct((1,), f32), V((T,...  122 us

profile of v4, /device:TPU:6, one launch (start us, length us, event | category | flops | bytes accessed | tf_op | source)
XLA Modules:
  0.0 126.6 jit_solution(12247016121915618360)
XLA Ops:
  1.3 121.7 %shard_map.76 = (f32[1]{0:T(128)}, f32[512,512]{1,0:T(8,128)S(1)}, f32[512,512]{1,0:T(8,128)S(1)}) custom-call(bf16[240,512]{1,0:T(8,128)(2,1)} %view1.1, bf16[240,512]{1,0:T(8,128)(2,1)} %view2.1, bf16[3840,512]{1,0:T(8,128)(2,1)} %in1.1, bf16[3840,512]{1,0:T(8,128)(2,1)} %in2.1, f32[1]{0:T(128)S(6)} %copy.13.scale_ref), custom_call_target="tpu_custom_call" | custom-call | flops 10066329600 | bytes 9961472 | tf_op jit(solution)/shard_map/pallas_call | solution.py:650
  123.0 1.0 copy.11
  124.0 1.0 copy.12

commit v5 on v4

--- a/solution.py
+++ b/solution.py
@@ -31,7 +31,8 @@
         XSLOT[key + (hop,)] = len(XSLOT)
 CORDER = [(0, 2), (1, 2), (1, 1), (0, 3), (0, 1), (1, 3), (1, 0), (0, 0)]
 CSLOT = {key: n for n, key in enumerate(CORDER)}
-NSEM = 240
+NSEM = 83
+FINAL = (("p", 0, 4), ("m", 0, 3), ("m", 1, 3))
 
 def both_z(r, hp, hm):
     return [("z", d, r, h, u) for u in range(NP) for d, h in (("p", hp), ("m", hm)) if h]
@@ -53,11 +54,11 @@
     both_z(0, 3, 3),
     [("x", "xp", 0, 2), ("x", "xm", 1, 2)] + over_y("p", 2) + [("ls", 1)],
     one_z("m", 1, 2),
-    [("c", r, dx) for r, dx in CORDER],
+    [("c",)],
     one_z("p", 0, 4),
     one_z("p", 1, 3),
     one_z("m", 1, 3),
-    [("lr", 0), ("lr", 1)],
+    [("lr",)],
     one_z("p", 1, 4),
 ]
 WHOLE = 7
@@ -161,37 +162,43 @@
     pl.semaphore_wait(barrier, len(peers))
 
     names = {}
-    flying = {}
 
     def index(name):
+        if name[0] in ("g", "d"):
+            name = ("gather",) + name[1:]
         return names.setdefault(name, len(names))
 
+    def group(name):
+        if name[0] in ("g", "d"):
+            return 0 if name[1] in ("yl", "xp", "xm", "c") else 1
+        if name[0] == "s":
+            return 2 if isinstance(name[1], tuple) else 3
+        return ("a1", "a2", "al").index(name[0]) + 4
+
     def send(name, src, dst, dev):
-        k = index(name)
-        copy = pltpu.make_async_remote_copy(
-            src_ref=src, dst_ref=dst, send_sem=ssem.at[k], recv_sem=rsem.at[k],
+        pltpu.make_async_remote_copy(
+            src_ref=src, dst_ref=dst, send_sem=ssem.at[group(name)], recv_sem=rsem.at[index(name)],
             device_id=dev, device_id_type=MESH,
-        )
-        copy.start()
-        flying[name] = copy
+        ).start()
 
     def recv(name, dst):
-        k = index(name)
         pltpu.make_async_remote_copy(
-            src_ref=dst, dst_ref=dst, send_sem=ssem.at[k], recv_sem=rsem.at[k],
+            src_ref=dst, dst_ref=dst, send_sem=ssem.at[0], recv_sem=rsem.at[index(name)],
             device_id=to_core, device_id_type=MESH,
         ).wait_recv()
 
-    def drain(keep=lambda name: True):
-        for name in [n for n in flying if keep(n)]:
-            flying.pop(name).wait_send()
+    def drain(which, ref):
+        pltpu.make_async_remote_copy(
+            src_ref=ref, dst_ref=ref, send_sem=ssem.at[which], recv_sem=rsem.at[0],
+            device_id=to_core, device_id_type=MESH,
+        ).wait_send()
 
     def start_a(tag, A, src):
         own = at(A, dp)
         send((tag, "yl"), src, own, to_yl)
         send((tag, "xp", 0, 1), src, own, to["xp"])
         send((tag, "xm", 0, 1), src, own, to["xm"])
-        send((tag, "c", 0, 0), src, own, to_core)
+        send((tag, "c"), src, own, to_core)
 
     def start_b(tag, Bb, src, u):
         for d in ("p", "m"):
@@ -202,24 +209,31 @@
         recv((tag, "yl"), at(A, i))
         send((tag, "xp", 1, 1), at(A, i), at(A, i), to["xp"])
         send((tag, "xm", 1, 1), at(A, i), at(A, i), to["xm"])
-        send((tag, "c", 1, 0), at(A, i), at(A, i), to_core)
+        send((tag, "c"), at(A, i), at(A, i), to_core)
         return i
+
+    def z_name(tag, d, r, h, u):
+        return (tag, d, r, h) if (d, r, h) in FINAL else (tag, d, r, h, u)
 
     def ev_z(tag, Bb, d, r, h, u):
         i = fti(r, -h if d == "p" else h)
+        if (d, r, h) in FINAL:
+            if u == 0:
+                recv((tag, d, r, h), at(Bb, i))
+            return i
         piece = at(Bb, i, u)
         recv((tag, d, r, h, u), piece)
         if r == 0 and (d, h) in (("m", 1), ("p", 2)):
             send((tag, "y", d, h, u), piece, piece, to_yh)
         if h < (4 if d == "p" else 3):
-            send((tag, d, r, h + 1, u), piece, piece, to[d])
+            send(z_name(tag, d, r, h + 1, u), piece, piece, to[d])
         return i
 
     def ev_y(tag, Bb, d, h, u):
         i = fti(1, -h if d == "p" else h)
         piece = at(Bb, i, u)
         recv((tag, "y", d, h, u), piece)
-        send((tag, d, 1, h + 1, u), piece, piece, to[d])
+        send(z_name(tag, d, 1, h + 1, u), piece, piece, to[d])
         return i
 
     def ev_x(tag, A, d, r, h):
@@ -228,60 +242,63 @@
         recv((tag, d, r, h), at(A, i))
         if h < KX[d, r]:
             send((tag, d, r, h + 1), at(A, i), at(A, i), to[d])
-        send((tag, "c", r, dx), at(A, i), at(A, i), to_core)
+        send((tag, "c"), at(A, i), at(A, i), to_core)
         return i
 
     def late_send(tag, Bb, n):
         block = at(Bb, fti(0, -n))
-        send((tag, "y", n), block, block, to_yh)
-
-    def late_recv(tag, Bb, n):
-        i = fti(1, -n)
-        recv((tag, "y", n), at(Bb, i))
-        return i
+        send((tag, "y"), block, block, to_yh)
 
     def gather(tag, A, Bb, hook_a, hook_b, after):
         last = len(PIECES) - 1
-        for n, group in enumerate(ORDER):
+        for n, steps in enumerate(ORDER):
             work = []
-            for kind, *args in group:
+            for kind, *args in steps:
                 if kind == "z" or kind == "y":
                     i = (ev_z if kind == "z" else ev_y)(tag, Bb, *args)
-                    if args[-1] == last:
+                    if n == len(ORDER) - 1:
+                        hook_b(i, args[-1])
+                    elif args[-1] == last:
                         work.append((hook_b, i))
                 elif kind == "ls":
                     late_send(tag, Bb, *args)
                 elif kind == "lr":
-                    work.append((hook_b, late_recv(tag, Bb, *args)))
+                    recv((tag, "y"), Bb.at[pl.ds(0, 2 * R)])
+                    work += [(hook_b, fti(1, 0)), (hook_b, fti(1, -1))]
                 elif kind == "yl":
                     work.append((hook_a, ev_yl(tag, A)))
                 elif kind == "x":
                     work.append((hook_a, ev_x(tag, A, *args)))
                 else:
-                    work.append((hook_a, ev_c(tag, A, *args)))
+                    recv((tag, "c"), A.at[pl.ds(0, len(CORDER) * R)])
+                    work += [(hook_a, dpi(r, dx, 1)) for r, dx in CORDER]
             for hook, i in work:
                 hook(i)
             if n in after:
                 after[n]()
 
-    def ev_c(tag, A, r, dx):
-        i = dpi(r, dx, 1)
-        recv((tag, "c", r, dx), at(A, i))
-        return i
-
     CH = 48
 
-    def moments(V, M, i):
-        base = i * R
+    def span(u):
+        return (0, R) if u is None else PIECES[u]
+
+    def moments(V, M, i, u=None):
+        start, count = span(u)
+        base = i * R + start
+        step = next(n for n in (48, 32, 16) if count % n == 0)
 
         def body(k, carry):
             s, q = carry
-            v = V[pl.ds(pl.multiple_of(base + k * CH, 16), CH), :].astype(f32)
+            v = V[pl.ds(pl.multiple_of(base + k * step, 16), step), :].astype(f32)
             return s + fold8(v), q + fold8(v * v)
 
-        s, q = lax.fori_loop(0, R // CH, body, (M[0:8, :], M[8:16, :]))
+        s, q = lax.fori_loop(0, count // step, body, (M[0:8, :], M[8:16, :]))
         M[0:8, :] = s
         M[8:16, :] = q
+
+    def piece_rows(i, u):
+        start, count = span(u)
+        return pl.ds(pl.multiple_of(i * R + start, 16), count)
 
     def statistics(M):
         average = jnp.sum(M[0:8, :], axis=0, keepdims=True) / B
@@ -315,13 +332,14 @@
     ready = []
     waiting = [ft]
 
-    def corr(i):
-        C[...] += dot_tn(V1[rows(i), :], V2[rows(i), :])
-
-    def work_two(i):
-        moments(V2, M2, i)
+    def corr(i, u=None):
+        at_ = piece_rows(i, u)
+        C[...] += dot_tn(V1[at_, :], V2[at_, :])
+
+    def work_two(i, u=None):
+        moments(V2, M2, i, u)
         if ready:
-            corr(i)
+            corr(i, u)
         else:
             waiting.append(i)
 
@@ -330,7 +348,7 @@
             corr(waiting.pop(0))
 
     def first_whole():
-        drain(lambda n: n[1] in ("c", "xp", "xm", "yl"))
+        drain(0, V1.at[pl.ds(0, 15 * R)])
         statistics(M1)
         normalize(V1, M1)
         C[...] = jnp.zeros_like(C)
@@ -471,13 +489,16 @@
         pair1(r, dx)
         slot = CSLOT[r, dx]
         cs[slot] = PT[rows(1 - c), :].astype(bf16)
-        send(("s", "c", r, dx), cs.at[slot], cr.at[slot], to_core)
+        send(("s", "c", slot >= 2), cs.at[slot], cr.at[slot], to_core)
 
     def both(r, dx):
         dx = dx % NX
         slot = CSLOT[r, dx]
         val = P1[slot]
-        recv(("s", "c", r, dx), cr.at[slot])
+        if slot == 0:
+            recv(("s", "c", False), cr.at[pl.ds(0, 2)])
+        if slot == 2:
+            recv(("s", "c", True), cr.at[pl.ds(2, 6)])
         return val + cr[slot].astype(f32)
 
     def xc(d, r, s):
@@ -501,7 +522,7 @@
 
     far(0)
     far(1)
-    drain(lambda n: n[0] == "g")
+    drain(1, V2.at[pl.ds(0, 15 * R)])
     normalize(V2, M2)
     pair2(-1)
     zc(0, 1, 1, True)
@@ -591,8 +612,9 @@
     local[2].wait()
     local[3].wait()
 
-    def weight(w_ref, X, D, i, first=False):
-        term = dot_tn(X[rows(i), :], D[rows(i), :])
+    def weight(w_ref, X, D, i, u=None, first=False):
+        at_ = piece_rows(i, u)
+        term = dot_tn(X[at_, :], D[at_, :])
         if first:
             w_ref[...] = term
         else:
@@ -615,11 +637,17 @@
         else:
             loss_ref[0] = jnp.sum(AL[4]) / F
 
-    weight(w2_ref, X2, D2, ft, True)
+    weight(w2_ref, X2, D2, ft, first=True)
     after = {0: lambda: loss_step(1), 2: lambda: loss_step(2), 4: lambda: loss_step(3), WHOLE: weights_one}
-    gather("d", D1, D2, lambda i: None, lambda i: weight(w2_ref, X2, D2, i), after)
-    drain()
-    assert len(names) <= NSEM
+    gather("d", D1, D2, lambda i: None, lambda i, u=None: weight(w2_ref, X2, D2, i, u), after)
+    drain(0, D1.at[pl.ds(0, 15 * R)])
+    drain(1, D2.at[pl.ds(0, 15 * R)])
+    drain(2, zs)
+    drain(3, zs)
+    drain(4, A1.at[pl.ds(0, 4)])
+    drain(5, A2.at[pl.ds(0, 4)])
+    drain(6, AL.at[pl.ds(0, 4)])
+    assert len(names) == NSEM, len(names)
 
 
 def per_device(view_one, view_two, inputs_one, inputs_two, loss_scale):
@@ -643,7 +671,7 @@
         V((5, 8, T + 128), f32), V((4, 8, T + 128), f32),
         V((5, 8, T), f32), V((4, 8, T), f32),
         V((5, 8, 128), f32), V((4, 8, 128), f32),
-        pltpu.SemaphoreType.DMA((NSEM,)),
+        pltpu.SemaphoreType.DMA((7,)),
         pltpu.SemaphoreType.DMA((NSEM,)),
         pltpu.SemaphoreType.DMA((4,)),
     ]

time: 128 us -> 124 us (0.969)
  Pallas kernels: 122 us -> 118 us
    pallas_call x1, Pallas kernels: 122 us -> 118 us  [per_device(): pl.pallas_call(kernel, out_shape=(jax.ShapeDtypeStruct((1,), f32), V((T,...]
where the time goes in v5:
time: 124 us; the launch traced here: 123 us
  Pallas kernels  118 us (95%)
  between operations  2.98 us (2%)
  local copies, waits for them, and re-layouts  1.94 us (2%)
    pallas_call x1, Pallas kernels, per_device(): pl.pallas_call(kernel, out_shape=(jax.ShapeDtypeStruct((1,), f32), V((T,...  118 us

profile of v5, /device:TPU:6, one launch (start us, length us, event | category | flops | bytes accessed | tf_op | source)
XLA Modules:
  0.0 123.0 jit_solution(928341096759882203)
XLA Ops:
  1.3 118.1 %shard_map.76 = (f32[1]{0:T(128)}, f32[512,512]{1,0:T(8,128)S(1)}, f32[512,512]{1,0:T(8,128)S(1)}) custom-call(bf16[240,512]{1,0:T(8,128)(2,1)} %view1.1, bf16[240,512]{1,0:T(8,128)(2,1)} %view2.1, bf16[3840,512]{1,0:T(8,128)(2,1)} %in1.1, bf16[3840,512]{1,0:T(8,128)(2,1)} %in2.1, f32[1]{0:T(128)S(6)} %copy.13.scale_ref), custom_call_target="tpu_custom_call" | custom-call | flops 10066329600 | bytes 9961472 | tf_op jit(solution)/shard_map/pallas_call | solution.py:678
  119.4 1.0 copy.11
  120.3 1.0 copy.12

commit v6 on v5

--- a/solution.py
+++ b/solution.py
@@ -55,8 +55,8 @@
     [("x", "xp", 0, 2), ("x", "xm", 1, 2)] + over_y("p", 2) + [("ls", 1)],
     one_z("m", 1, 2),
     [("c",)],
+    one_z("p", 1, 3),
     one_z("p", 0, 4),
-    one_z("p", 1, 3),
     one_z("m", 1, 3),
     [("lr",)],
     one_z("p", 1, 4),
@@ -353,9 +353,9 @@
         normalize(V1, M1)
         C[...] = jnp.zeros_like(C)
         ready.append(True)
-        some(4)
-
-    after = {WHOLE: first_whole, WHOLE + 1: lambda: some(2), WHOLE + 2: lambda: some(4), WHOLE + 3: lambda: some(20)}
+        some(3)
+
+    after = {WHOLE: first_whole, WHOLE + 1: lambda: some(3), WHOLE + 2: lambda: some(5), WHOLE + 3: lambda: some(20)}
     gather("g", V1, V2, lambda i: moments(V1, M1, i), work_two, after)
     statistics(M2)
 
@@ -378,33 +378,34 @@
     row0 = ft * T
     col0 = dp * T
 
-    def grad(k, loss):
+    def tile(k):
         at_ = pl.ds(pl.multiple_of(k * CG, CG), CG)
         corr_ = C[at_, :] * inv_two
         row_ids = row0 + k * CG + lax.broadcasted_iota(jnp.int32, (CG, T), 0)
         col_ids = col0 + lax.broadcasted_iota(jnp.int32, (CG, T), 1)
-        on = row_ids == col_ids
-        miss = 1.0 - corr_
-        loss = loss + fold8(jnp.where(on, miss * miss, off_weight * corr_ * corr_))
-        g = (jnp.where(on, -2.0 * miss, 2.0 * off_weight * corr_) * scale).astype(bf16)
-        G[at_, :] = g
-        prod = g.astype(f32) * corr_
+        return at_, corr_, row_ids == col_ids, 1.0 - corr_
+
+    def grad(k, carry):
+        at_, corr_, on, miss = tile(k)
+        G[at_, :] = (jnp.where(on, -2.0 * miss, 2.0 * off_weight * corr_) * scale).astype(bf16)
+        return carry
+
+    lax.fori_loop(0, T // CG, grad, 0)
+
+    def terms(k, loss):
+        at_, corr_, on, miss = tile(k)
+        prod = G[at_, :].astype(f32) * corr_
         high = prod.astype(bf16)
         GH[at_, :] = high
         GL[at_, :] = (prod - high.astype(f32)).astype(bf16)
-        return loss
-
-    loss = lax.fori_loop(0, T // CG, grad, jnp.zeros((8, T), f32))
-    loss_tile = loss[:, 0:128]
-    for k in range(128, T, 128):
-        loss_tile = loss_tile + loss[:, k : k + 128]
+        return loss + fold8(jnp.where(on, miss * miss, off_weight * corr_ * corr_))
 
     DC = 16
 
     def delta(U, V, M, A, D, i, start, count):
         stats = A[4]
-        first = stats[0:1, 0:T] / B
-        second = stats[1:2, 0:T] / B
+        first = jnp.concatenate([stats[k : k + 1] for k in range(4)], axis=1) / B
+        second = jnp.concatenate([stats[k : k + 1] for k in range(4, 8)], axis=1) / B
         inv = M[16:17, :]
 
         def body(k, carry):
@@ -452,8 +453,9 @@
     def far(u):
         if u == 0:
             pair2(-4)
+        zc(u, 1, 4)
+        if u == 0:
             pair2(3)
-        zc(u, 1, 4)
         zc(u, 1, -3)
 
     def far_own(u):
@@ -537,6 +539,25 @@
     for r, dx in CORDER[4:8]:
         core_send(r, dx)
     far_own(1)
+    cross(0)
+    xc("xp", 1, 0)
+    xc("xm", 0, 0)
+    cross(1)
+    middle_own(0)
+    def put(n):
+        send(("a1", n), A1.at[n], R1.at[n], dp_steps[n])
+        send(("a2", n), A2.at[n], R2.at[n], feat_steps[n])
+
+    def take(n):
+        recv(("a1", n), R1.at[n])
+        recv(("a2", n), R2.at[n])
+        A1[n + 1] = A1[n] + R1[n]
+        A2[n + 1] = A2[n] + R2[n]
+
+    loss = lax.fori_loop(0, T // CG, terms, jnp.zeros((8, T), f32))
+    loss_tile = loss[:, 0:128]
+    for k in range(128, T, 128):
+        loss_tile = loss_tile + loss[:, k : k + 128]
 
     ones = jnp.ones((16, T), bf16)
     second1 = dot_nt(ones, GH[...]) + dot_nt(ones, GL[...])
@@ -550,51 +571,44 @@
 
     first1 = jnp.sum(dot_nt(split_rows(M2), G[...]), axis=0, keepdims=True) / B
     first2 = jnp.sum(dot_nn(split_rows(M1), G[...]), axis=0, keepdims=True) / B
-    top = lane_row[0:8] == 0
-    A1[0, :, 0:T] = jnp.where(top, jnp.broadcast_to(first1, (8, T)), second1[0:8])
-    A1[0, :, T : T + 128] = loss_tile
-    A2[0] = jnp.where(top, jnp.broadcast_to(first2, (8, T)), second2[0:8])
-
-    def put(n):
-        send(("a1", n), A1.at[n], R1.at[n], dp_steps[n])
-        send(("a2", n), A2.at[n], R2.at[n], feat_steps[n])
-
-    def take(n):
-        recv(("a1", n), R1.at[n])
-        recv(("a2", n), R2.at[n])
-        A1[n + 1] = A1[n] + R1[n]
-        A2[n + 1] = A2[n] + R2[n]
+
+    for k in range(T // 128):
+        lanes = slice(k * 128, k * 128 + 128)
+        A1[0, k : k + 1, :] = first1[:, lanes]
+        A1[0, 4 + k : 5 + k, :] = second1[0:1, lanes]
+        A2[0, k : k + 1, :] = first2[:, lanes]
+        A2[0, 4 + k : 5 + k, :] = second2[0:1, lanes]
+    A1[0, 8:16, :] = loss_tile
 
     put(0)
-    cross(0)
-    xc("xp", 1, 0)
-    xc("xm", 0, 0)
-    middle_own(0)
-    take(0)
-    put(1)
-    cross(1)
     middle_own(1)
     xc("xp", 0, 1)
     xc("xm", 1, 1)
-    take(1)
-    put(2)
     pair2(0)
     zc(0, 1, 0, True)
     zc(1, 1, 0, True)
+    take(0)
+    put(1)
     near(0)
+    near(1)
+    take(1)
+    put(2)
+    ys[0] = x_end(1).astype(bf16)
+    send(("s", "yl"), ys.at[0], yr.at[0], to_yl)
     take(2)
     put(3)
-    ys[0] = x_end(1).astype(bf16)
-    send(("s", "yl"), ys.at[0], yr.at[0], to_yl)
-    near(1)
+
+    nearest(0)
     take(3)
-    nearest(0)
+    nearest(1)
+    z_end(0)
     val = x_end(0)
     recv(("s", "yl"), yr.at[0])
     U1[...] = val + yr[0].astype(f32)
     delta(U1, V1, M1, A1, D1, dp, 0, R)
     start_a("d", D1, at(D1, dp))
-    AL[0] = A1[4, :, T : T + 128]
+    z_end(1)
+    AL[0] = A1[4, 8:16, :]
 
     def put_l(n):
         send(("al", n), AL.at[n], RL.at[n], feat_steps[n])
@@ -604,11 +618,9 @@
         AL[n + 1] = AL[n] + RL[n]
 
     put_l(0)
-    nearest(1)
-    z_end(0)
     take_l(0)
     put_l(1)
-    z_end(1)
+
     local[2].wait()
     local[3].wait()
 
@@ -668,8 +680,8 @@
         V(block, f32), V(block, f32),
         V((T, T), f32), V((T, T), bf16), V((T, T), bf16), V((T, T), bf16),
         V((40, T), f32), V((40, T), f32),
-        V((5, 8, T + 128), f32), V((4, 8, T + 128), f32),
-        V((5, 8, T), f32), V((4, 8, T), f32),
+        V((5, 16, 128), f32), V((4, 16, 128), f32),
+        V((5, 8, 128), f32), V((4, 8, 128), f32),
         V((5, 8, 128), f32), V((4, 8, 128), f32),
         pltpu.SemaphoreType.DMA((7,)),
         pltpu.SemaphoreType.DMA((NSEM,)),

time: 124 us -> 123 us (level)
  no operation moved by 1% of the time
where the time goes in v6:
time: 123 us; the launch traced here: 122 us
  Pallas kernels  117 us (95%)
  between operations  2.98 us (2%)
  local copies, waits for them, and re-layouts  1.94 us (2%)
    pallas_call x1, Pallas kernels, per_device(): pl.pallas_call(kernel, out_shape=(jax.ShapeDtypeStruct((1,), f32), V((T,...  117 us

profile of v6, /device:TPU:6, one launch (start us, length us, event | category | flops | bytes accessed | tf_op | source)
XLA Modules:
  0.0 122.0 jit_solution(2778346086092155529)
XLA Ops:
  1.3 117.1 %shard_map.76 = (f32[1]{0:T(128)}, f32[512,512]{1,0:T(8,128)S(1)}, f32[512,512]{1,0:T(8,128)S(1)}) custom-call(bf16[240,512]{1,0:T(8,128)(2,1)} %view1.1, bf16[240,512]{1,0:T(8,128)(2,1)} %view2.1, bf16[3840,512]{1,0:T(8,128)(2,1)} %in1.1, bf16[3840,512]{1,0:T(8,128)(2,1)} %in2.1, f32[1]{0:T(128)S(6)} %copy.13.scale_ref), custom_call_target="tpu_custom_call" | custom-call | flops 10066329600 | bytes 9961472 | tf_op jit(solution)/shard_map/pallas_call | solution.py:690
  118.4 1.0 copy.11
  119.4 1.0 copy.12

commit v7 on v6

--- a/solution.py
+++ b/solution.py
@@ -529,6 +529,9 @@
     pair2(-1)
     zc(0, 1, 1, True)
     zc(1, 1, 1, True)
+    pair2(0)
+    zc(0, 1, 0, True)
+    zc(1, 1, 0, True)
     for r, dx in CORDER[0:4]:
         core_send(r, dx)
     middle(0)
@@ -584,9 +587,6 @@
     middle_own(1)
     xc("xp", 0, 1)
     xc("xm", 1, 1)
-    pair2(0)
-    zc(0, 1, 0, True)
-    zc(1, 1, 0, True)
     take(0)
     put(1)
     near(0)

time: 123 us -> 123 us (level)
  no operation moved by 1% of the time
where the time goes in v7:
time: 123 us
  Pallas kernels  118 us (96%)
  between operations  2.98 us (2%)
  local copies, waits for them, and re-layouts  1.94 us (2%)
    pallas_call x1, Pallas kernels, per_device(): pl.pallas_call(kernel, out_shape=(jax.ShapeDtypeStruct((1,), f32), V((T,...  118 us

profile of v7, /device:TPU:6, one launch (start us, length us, event | category | flops | bytes accessed | tf_op | source)
XLA Modules:
  0.0 122.5 jit_solution(15122126020462901989)
XLA Ops:
  1.3 117.6 %shard_map.76 = (f32[1]{0:T(128)}, f32[512,512]{1,0:T(8,128)S(1)}, f32[512,512]{1,0:T(8,128)S(1)}) custom-call(bf16[240,512]{1,0:T(8,128)(2,1)} %view1.1, bf16[240,512]{1,0:T(8,128)(2,1)} %view2.1, bf16[3840,512]{1,0:T(8,128)(2,1)} %in1.1, bf16[3840,512]{1,0:T(8,128)(2,1)} %in2.1, f32[1]{0:T(128)S(6)} %copy.13.scale_ref), custom_call_target="tpu_custom_call" | custom-call | flops 10066329600 | bytes 9961472 | tf_op jit(solution)/shard_map/pallas_call | solution.py:690
  118.9 1.0 copy.11
  119.9 1.0 copy.12
